TPU v7x, 512 devices: a whole 4x4x16 slice. The times are simulated.
512 devices in a mesh: section: 8 (over x, core), store: 64 (over y, z).
Axes of the slice: x: 4, y: 4, z: 16, core: 2. Of those that a mesh axis runs over, the one named last changes fastest.
Arguments:
- hidden_in: bfloat16 [8, 1536, 3584], P('section', 'store'), may hold values from -6 to 6
- incoming: bfloat16 [1536, 3584], P('store'), may hold values from -6 to 6
- routes: int32 [2, 8, 1536, 2], P(None, 'section', 'store'), may hold values from 0 to 7, all different within a row; in each aligned block of 24 rows (0 to 23, 24 to 47, ..., all dimensions but the last counted through in order) at most 8 rows name the same one
- gates: float32 [2, 8, 1536, 2], P(None, 'section', 'store'), may hold values from 0.2 to 2
- norm_gain: float32 [8, 3584], P('section'), may hold values from 0.1 to 1.9
- w_gate: bfloat16 [8, 3584, 8192], P('section', None, 'store'), may hold values from -0.09375 to 0.09375
- w_up: bfloat16 [8, 3584, 8192], P('section', None, 'store'), may hold values from -0.09375 to 0.09375
- w_down: bfloat16 [8, 8192, 3584], P('section', 'store'), may hold values from -0.1875 to 0.1875
Outputs:
- after_first: bfloat16 [8, 1536, 3584], P('section', 'store')
- after_second: bfloat16 [8, 1536, 3584], P('section', 'store')
Inputs may be any that keep to these rules, and one draw needn't show every extreme that they name: `routes`: each row names 2 different experts; among the rows of one device (aligned blocks of 24 rows) no expert is named more than 8 times, a bound that some block reaches.
All inputs are finite; a program needn't handle non-finite values.
Results may differ from a plain program's by a relative error of at most 0.018.
Values may be sent and summed in bfloat16 or wider, within the bound.
No kernel may reach another device: no remote copies, remote signals or barrier semaphores. Data moves between devices by JAX's collectives and lax.ppermute only.
A program may use at most 64 MiB of HBM per device.

v0:
```python
import jax
import jax.numpy as jnp
from jax import lax
from jax.sharding import PartitionSpec as P

TOPK = 2
HS = 8


HIGH = lax.Precision.HIGHEST


def shifted(shard, axis, by):
    peers = lax.axis_size(axis)
    pairs = [(i, i + by) for i in range(peers) if 0 <= i + by < peers]
    return lax.ppermute(shard, axis, pairs)


def norm_rows(acts, gain):
    values = acts.astype(jnp.float32)
    scale = lax.rsqrt(jnp.mean(values * values, axis=-1, keepdims=True) + 1e-06)
    return ((values * scale * gain).astype(jnp.bfloat16), values)


def slot_tables(picks, weights, experts, capacity):
    rows, topk = picks.shape
    flat = picks.reshape(-1)
    onehot = (flat[:, None] == jnp.arange(experts, dtype=jnp.int32)[None, :]).astype(jnp.int32)
    before = jnp.cumsum(onehot, axis=0) - onehot
    position = jnp.sum(before * onehot, axis=1)
    slot = flat * capacity + position
    chosen = (slot[:, None] == jnp.arange(experts * capacity, dtype=jnp.int32)[None, :]).astype(
        jnp.float32
    )
    chosen = chosen.reshape(rows, topk, experts * capacity)
    dispatch = jnp.sum(chosen, axis=1)
    combine = jnp.sum(chosen * weights[:, :, None], axis=1)
    return (dispatch, combine)


def expert_rows(rows, gate_w, up_w, down_w):
    gate = jnp.dot(rows, gate_w, preferred_element_type=jnp.float32)
    upper = jnp.dot(rows, up_w, preferred_element_type=jnp.float32)
    hidden = (jax.nn.silu(gate) * upper).astype(jnp.bfloat16)
    return jnp.dot(hidden, down_w, preferred_element_type=jnp.float32).astype(jnp.bfloat16)


def layer(acts, picks, weights, gain, gate_w, up_w, down_w):
    rows, width = acts.shape
    n_store = lax.axis_size("store")
    experts = n_store // HS
    capacity = HS * ((rows * TOPK + experts * HS - 1) // (experts * HS))
    normed, values = norm_rows(acts, gain)
    dispatch, combine = slot_tables(picks, weights, experts, capacity)
    packed = jnp.einsum(
        "rs,rd->sd", dispatch.astype(jnp.bfloat16), normed, preferred_element_type=jnp.float32
    ).astype(jnp.bfloat16)
    outgoing = jnp.broadcast_to(
        packed.reshape(experts, 1, capacity, width), (experts, HS, capacity, width)
    ).reshape(n_store, capacity, width)
    received = lax.all_to_all(outgoing, "store", split_axis=0, concat_axis=0, tiled=True)
    shape = received.shape
    partial_out = expert_rows(received.reshape(-1, width), gate_w, up_w, down_w).reshape(shape)
    returned = lax.all_to_all(partial_out, "store", split_axis=0, concat_axis=0, tiled=True)
    summed = jnp.sum(returned.reshape(experts, HS, capacity, width).astype(jnp.float32), axis=1)
    mixed = jnp.dot(combine, summed.reshape(experts * capacity, width), precision=HIGH)
    return (values + mixed).astype(jnp.bfloat16)


def on_device(hidden_in, incoming, routes, gates, norm_gain, w_gate, w_up, w_down):
    section_place = lax.axis_index("section")
    first = layer(
        hidden_in[0], routes[0, 0], gates[0, 0], norm_gain[0], w_gate[0], w_up[0], w_down[0]
    )
    handed = shifted(first, "section", 1)
    entry = jnp.where(section_place == 0, incoming, handed)
    second = layer(entry, routes[1, 0], gates[1, 0], norm_gain[0], w_gate[0], w_up[0], w_down[0])
    return (first[None], second[None])


def solution(mesh):
    placed = (
        P("section", "store", None),
        P("store", None),
        P(None, "section", "store", None),
        P(None, "section", "store", None),
        P("section", None),
        P("section", None, "store"),
        P("section", None, "store"),
        P("section", "store", None),
    )
    return jax.shard_map(
        on_device,
        mesh=mesh,
        in_specs=placed,
        out_specs=(P("section", "store", None), P("section", "store", None)),
        check_vma=False,
    )
```

profile of v0, /device:TPU:26, one launch (start us, length us, event | category | flops | bytes accessed | tf_op | source)
XLA Modules:
  0.0 742.1 jit_solution(12129058335358182168)
XLA Ops:
  0.6 0.0 copy-start
  0.6 1.1 fusion.46
  1.8 0.7 slice_bitcast_fusion
  2.5 0.7 fusion.74
  3.2 0.1 copy.28
  3.3 0.1 eq.69
  3.4 0.1 copy.26
  3.5 0.1 eq.61
  3.6 0.1 fusion.69
  3.6 0.1 reduce_window_sum.17
  3.7 0.2 select_reduce_fusion.3
  3.9 0.1 reduce_sum.95
  4.0 0.1 copy.27
  4.1 0.1 fusion.68
  4.2 0.1 reduce_window_sum.18
  4.2 0.2 select_reduce_fusion.1
  4.4 0.1 reduce_sum.101
  4.5 0.1 copy.29
  4.6 0.8 reduce
  5.4 0.7 bitcast_add_fusion
  6.1 0.1 convert_reduce_fusion.3
  6.2 1.2 fusion.2
  7.4 0.3 broadcast_in_dim.13
  7.7 0.0 copy-start.4
  7.7 184.1 %all_to_all.20 = bf16[64,8,3584]{2,1,0:T(8,128)(2,1)S(1)} all-to-all(bf16[64,8,3584]{2,1,0:T(8,128)(2,1)S(1)} %bitcast.90), channel_id=1, replica_groups=mesh['section'=8,'store'=64] {'store'}, dimensions={0} | all-to-all | bytes 7340032 | tf_op jit(solution)/shard_map/all_to_all | solution.py:61
  191.9 1.8 copy-done.1
  193.6 0.0 copy-done.4
  193.7 1.1 fusion.13
  194.8 0.1 copy-done.3
  194.8 7.8 %fusion = bf16[64,8,3584]{2,1,0:T(8,128)(2,1)} fusion(bf16[1,128,3584]{2,1,0:T(8,128)(2,1)S(1)} %copy-done, bf16[64,8,3584]{2,1,0:T(8,128)(2,1)} %copy-done.1, bf16[1,3584,128]{2,1,0:T(8,128)(2,1)S(1)} %copy-done.3, f32[512,128]{1,0:T(8,128)S(1)} %fusion.13), kind=kOutput, calls=%fused_computation.4 | convolution fusion | flops 941752320 | bytes 9437184 | tf_op jit(solution)/shard_map/dot_general | solution.py:45
  202.6 172.8 %all_to_all.21 = bf16[64,8,3584]{2,1,0:T(8,128)(2,1)S(1)} all-to-all(bf16[64,8,3584]{2,1,0:T(8,128)(2,1)} %fusion), channel_id=1, replica_groups=mesh['section'=8,'store'=64] {'store'}, dimensions={0} | all-to-all | bytes 7340032 | tf_op jit(solution)/shard_map/all_to_all | solution.py:64
  375.4 0.5 convert_reduce_fusion.1
  375.9 0.4 copy-done.5
  376.3 0.6 fusion.4
  376.9 0.0 copy-start.6
  376.9 1.9 collective-permute-start
  378.8 0.1 convert_reduce_fusion.2
  378.9 4.7 collective-permute-done
  383.6 0.2 fusion.43
  383.8 0.3 fusion.3
  384.2 0.3 broadcast_in_dim.32
  384.4 173.0 %all_to_all.22 = bf16[64,8,3584]{2,1,0:T(8,128)(2,1)S(1)} all-to-all(bf16[64,8,3584]{2,1,0:T(8,128)(2,1)S(1)} %bitcast.91), channel_id=1, replica_groups=mesh['section'=8,'store'=64] {'store'}, dimensions={0} | all-to-all | bytes 7340032 | tf_op jit(solution)/shard_map/all_to_all | solution.py:61
  557.4 1.8 copy-done.2
  559.2 1.1 fusion.9
  560.4 7.8 %fusion.1 = bf16[64,8,3584]{2,1,0:T(8,128)(2,1)} fusion(bf16[1,128,3584]{2,1,0:T(8,128)(2,1)S(1)} %copy-done, bf16[64,8,3584]{2,1,0:T(8,128)(2,1)} %copy-done.2, bf16[1,3584,128]{2,1,0:T(8,128)(2,1)S(1)} %copy-done.3, f32[512,128]{1,0:T(8,128)S(1)} %fusion.9), kind=kOutput, calls=%fused_computation.5 | convolution fusion | flops 941752320 | bytes 9437184 | tf_op jit(solution)/shard_map/dot_general | solution.py:45
  568.2 172.2 %all_to_all.23 = bf16[64,8,3584]{2,1,0:T(8,128)(2,1)S(1)} all-to-all(bf16[64,8,3584]{2,1,0:T(8,128)(2,1)} %fusion.1), channel_id=1, replica_groups=mesh['section'=8,'store'=64] {'store'}, dimensions={0} | all-to-all | bytes 7340032 | tf_op jit(solution)/shard_map/all_to_all | solution.py:64
  740.3 0.5 convert_reduce_fusion
  740.8 1.2 fusion.6
  (10 shorter events, 0.0 us)
Async XLA Ops:
  0.6 194.1 %copy-start = (bf16[1,128,3584]{2,1,0:T(8,128)(2,1)S(1)}, bf16[1,128,3584]{2,1,0:T(8,128)(2,1)}, u32[]{:S(2)}) copy-start(bf16[1,128,3584]{2,1,0:T(8,128)(2,1)} %param.15) | copy-start | bytes 2752516
  7.7 186.0 %copy-start.4 = (bf16[1,3584,128]{2,1,0:T(8,128)(2,1)S(1)}, bf16[1,3584,128]{2,1,0:T(8,128)(2,1)}, u32[]{:S(2)}) copy-start(bf16[1,3584,128]{2,1,0:T(8,128)(2,1)} %param.13) | copy-start | bytes 2752516
  191.9 1.8 copy-start.1
  193.7 1.2 copy-start.3
  375.4 0.9 copy-start.5
  375.4 8.2 %copy-start.7 = (bf16[24,3584]{1,0:T(8,128)(2,1)S(1)}, bf16[24,3584]{1,0:T(8,128)(2,1)}, u32[]{:S(2)}) copy-start(bf16[24,3584]{1,0:T(8,128)(2,1)} %param.9) | copy-start | bytes 516100
  376.9 180.5 %copy-start.6 = (bf16[24,3584]{1,0:T(8,128)(2,1)}, bf16[24,3584]{1,0:T(8,128)(2,1)S(1)}, u32[]{:S(2)}) copy-start(bf16[24,3584]{1,0:T(8,128)(2,1)S(1)} %fusion.4) | copy-start | bytes 516100
  376.9 6.7 collective-permute-start
  557.4 1.8 copy-start.2
where the time goes:
time: 743 us; the launch traced here: 742 us
  blocking collectives  702 us (94%)
  matrix products  21.2 us (3%)
    all_to_all x2, blocking collectives, layer(): lax.all_to_all(outgoing, 'store', split_axis=0, concat_axis=0, tiled=True)  357 us
    all_to_all x2, blocking collectives, layer(): lax.all_to_all(partial_out, 'store', split_axis=0, concat_axis=0, tiled=T...  345 us
    dot_general x2, matrix products, expert_rows(): jnp.dot(hidden, down_w, preferred_element_type=jnp.float32)  15.6 us
  transfers between devices with their start and end apart: 1, of which 1 were waited for; matrix products, arithmetic and copies ran while one was open for 0% of the time, Pallas kernels for 0%

commit v1 on v0

v1 whole, which is shorter than its diff:
```python
import jax
import jax.numpy as jnp
from jax import lax
from jax.sharding import Mesh, PartitionSpec as P

TOPK = 2
HS = 8
QUARTERS = 4


HIGH = lax.Precision.HIGHEST
STORE = ("y", "q", "b")


def shifted(shard, axis, by):
    peers = lax.axis_size(axis)
    pairs = [(i, i + by) for i in range(peers) if 0 <= i + by < peers]
    return lax.ppermute(shard, axis, pairs)


def swap(blocks, axis):
    return lax.all_to_all(blocks, axis, split_axis=0, concat_axis=0, tiled=True)


def norm_rows(acts, gain):
    values = acts.astype(jnp.float32)
    scale = lax.rsqrt(jnp.mean(values * values, axis=-1, keepdims=True) + 1e-06)
    return ((values * scale * gain).astype(jnp.bfloat16), values)


def slot_tables(picks, weights, experts, capacity):
    rows, topk = picks.shape
    flat = picks.reshape(-1)
    onehot = (flat[:, None] == jnp.arange(experts, dtype=jnp.int32)[None, :]).astype(jnp.int32)
    before = jnp.cumsum(onehot, axis=0) - onehot
    position = jnp.sum(before * onehot, axis=1)
    slot = flat * capacity + position
    chosen = (slot[:, None] == jnp.arange(experts * capacity, dtype=jnp.int32)[None, :]).astype(
        jnp.float32
    )
    chosen = chosen.reshape(rows, topk, experts * capacity)
    dispatch = jnp.sum(chosen, axis=1)
    combine = jnp.sum(chosen * weights[:, :, None], axis=1)
    return (dispatch, combine)


def layer(acts, tables, gain, in_w, out_w):
    dispatch, combine = tables
    rows, width = acts.shape
    n_store = lax.axis_size(STORE)
    experts = n_store // HS
    capacity = dispatch.shape[1] // experts
    part = width // QUARTERS
    halves = HS // QUARTERS
    normed, values = norm_rows(acts, gain)
    packed = jnp.einsum(
        "rep,rbf->ebpf",
        dispatch.astype(jnp.bfloat16).reshape(rows, experts, capacity),
        normed.reshape(rows, QUARTERS, part),
        preferred_element_type=jnp.float32,
    ).astype(jnp.bfloat16)
    outgoing = jnp.broadcast_to(
        packed[:, None], (experts, halves, QUARTERS, capacity, part)
    ).reshape(n_store, capacity, part)
    received = swap(outgoing, STORE).reshape(-1, part)
    partial_in = jnp.einsum(
        "rf,bfh->brh", received, in_w, preferred_element_type=jnp.float32
    ).astype(jnp.bfloat16)
    sums = jnp.sum(swap(partial_in, "b").astype(jnp.float32), axis=0)
    mine = sums.shape[1] // 2
    hidden = (jax.nn.silu(sums[:, :mine]) * sums[:, mine:]).astype(jnp.bfloat16)
    hidden = lax.all_gather(hidden, "b", axis=0)
    partial_out = jnp.einsum(
        "brh,bhf->rf", hidden, out_w, preferred_element_type=jnp.float32
    ).astype(jnp.bfloat16)
    returned = swap(partial_out.reshape(n_store, capacity, part), STORE)
    returned = returned.reshape(experts, halves, QUARTERS, capacity, part)
    summed = jnp.sum(returned.astype(jnp.float32), axis=1)
    mixed = jnp.einsum(
        "rep,ebpf->rbf", combine.reshape(rows, experts, capacity), summed, precision=HIGH
    ).reshape(rows, width)
    return (values + mixed).astype(jnp.bfloat16)


def on_device(hidden_in, incoming, routes, gates, norm_gain, w_gate, w_up, w_down):
    section_place = lax.axis_index("section")
    rows, width = incoming.shape
    n_store = lax.axis_size(STORE)
    experts = n_store // HS
    capacity = HS * ((rows * TOPK + experts * HS - 1) // (experts * HS))
    part = width // QUARTERS
    in_w = jnp.concatenate([w_gate[0], w_up[0]], axis=1).reshape(QUARTERS, part, -1)
    in_w = swap(in_w, "b")
    out_w = w_down[0].reshape(-1, QUARTERS, part).transpose(1, 0, 2)
    out_w = swap(out_w, "b")
    tables = [slot_tables(routes[t, 0], gates[t, 0], experts, capacity) for t in range(2)]
    first = layer(hidden_in[0], tables[0], norm_gain[0], in_w, out_w)
    handed = shifted(first, "section", 1)
    entry = jnp.where(section_place == 0, incoming, handed)
    second = layer(entry, tables[1], norm_gain[0], in_w, out_w)
    return (first[None], second[None])


def solution(mesh):
    sections, stores = mesh.devices.shape
    fine = Mesh(
        mesh.devices.reshape(sections, 4, stores // (4 * QUARTERS), QUARTERS),
        ("section",) + STORE,
    )
    placed = (
        P("section", STORE, None),
        P(STORE, None),
        P(None, "section", STORE, None),
        P(None, "section", STORE, None),
        P("section", None),
        P("section", None, STORE),
        P("section", None, STORE),
        P("section", STORE, None),
    )
    return jax.shard_map(
        on_device,
        mesh=fine,
        in_specs=placed,
        out_specs=(P("section", STORE, None), P("section", STORE, None)),
        check_vma=False,
    )
```

time: 743 us -> 409 us (0.55)
  the two profiles are of different devices: /device:TPU:26 before, /device:TPU:34 now
where the time goes in v1:
time: 409 us; the launch traced here: 408 us
  blocking collectives  169 us (41%)
  waiting for transfers between devices  159 us (39%)
  starting transfers between devices  53.2 us (13%)
  matrix products  10.4 us (3%)
  local copies, waits for them, and re-layouts  9.37 us (2%)
  other arithmetic  6.66 us (2%)
    all_to_all x5, waiting for transfers between devices, swap(): return lax.all_to_all(blocks, axis, split_axis=0, concat_axis=0, tiled=True)  154 us
    all_to_all x3, blocking collectives, swap(): return lax.all_to_all(blocks, axis, split_axis=0, concat_axis=0, tiled=True)  122 us
    all_to_all x5, starting transfers between devices, swap(): return lax.all_to_all(blocks, axis, split_axis=0, concat_axis=0, tiled=True)  51.3 us
    all_gather x2, blocking collectives, layer(): hidden = lax.all_gather(hidden, 'b', axis=0)  47.4 us
  transfers between devices with their start and end apart: 6, of which 5 were waited for; matrix products, arithmetic and copies ran while one was open for 1% of the time, Pallas kernels for 0%

profile of v1, /device:TPU:34, one launch (start us, length us, event | category | flops | bytes accessed | tf_op | source)
XLA Modules:
  0.0 408.5 jit_solution(10880060397774062176)
XLA Ops:
  0.6 0.7 fusion.30
  1.7 0.2 select_reduce_fusion.3
  2.1 0.1 eq.69
  2.4 0.2 select_reduce_fusion.1
  2.8 0.7 slice_bitcast_fusion
  3.5 0.7 bitcast_add_fusion
  4.4 1.1 fusion.14
  5.4 0.8 reduce
  6.2 1.0 fusion.16
  7.3 0.3 fusion.9
  7.6 1.0 broadcast_in_dim.8
  8.6 18.7 %all-to-all-start.1 = ((bf16[64,8,896]{2,1,0:T(8,128)(2,1)}), bf16[64,8,896]{2,1,0:T(8,128)(2,1)}, u32[]{:S(2)}, u32[]{:S(2)}) async-start(bf16[64,8,896]{2,1,0:T(8,128)(2,1)} %bitcast.10), calls=%async_computation.1 | async-start | bytes 1835008 | tf_op jit(solution)/shard_map/all_to_all | solution.py:22
  27.3 0.6 copy.77
  27.9 1.3 copy.78
  29.3 1.3 pad_maximum_fusion
  30.6 44.8 %all-to-all-done.1 = bf16[64,8,896]{2,1,0:T(8,128)(2,1)} async-done(((bf16[64,8,896]{2,1,0:T(8,128)(2,1)}), bf16[64,8,896]{2,1,0:T(8,128)(2,1)}, u32[]{:S(2)}, u32[]{:S(2)}) %all-to-all-start.1) | async-done | bytes 917536 | tf_op jit(solution)/shard_map/all_to_all | solution.py:22
  75.4 42.6 %all_to_all.40 = bf16[4,896,256]{1,2,0:T(8,128)(2,1)S(1)} all-to-all(bf16[4,896,256]{1,2,0:T(8,128)(2,1)S(1)} %pad_maximum_fusion), channel_id=1, replica_groups=mesh['section'=8,'y'=4,'q'=4,'b'=4] {'b'}, dimensions={0} | all-to-all | bytes 3670016 | tf_op jit(solution)/shard_map/all_to_all | solution.py:22
  117.9 1.3 copy-done
  119.2 3.5 fusion.5
  122.7 5.4 %all-to-all-start.2 = ((bf16[4,512,256]{1,2,0:T(8,128)(2,1)}), bf16[4,512,256]{1,2,0:T(8,128)(2,1)S(1)}, u32[]{:S(2)}, u32[]{:S(2)}) async-start(bf16[4,512,256]{1,2,0:T(8,128)(2,1)} %fusion.5), calls=%async_computation.2 | async-start | bytes 2097152 | tf_op jit(solution)/shard_map/all_to_all | solution.py:22
  128.1 0.6 copy.83
  128.7 1.3 copy.84
  130.0 19.4 %all-to-all-done.2 = bf16[4,512,256]{1,2,0:T(8,128)(2,1)S(1)} async-done(((bf16[4,512,256]{1,2,0:T(8,128)(2,1)}), bf16[4,512,256]{1,2,0:T(8,128)(2,1)S(1)}, u32[]{:S(2)}, u32[]{:S(2)}) %all-to-all-start.2) | async-done | bytes 1048608 | tf_op jit(solution)/shard_map/all_to_all | solution.py:22
  149.4 6.7 %all-to-all-start.3 = ((bf16[4,128,896]{2,1,0:T(8,128)(2,1)}), bf16[4,128,896]{2,1,0:T(8,128)(2,1)S(1)}, u32[]{:S(2)}, u32[]{:S(2)}) async-start(bf16[4,128,896]{2,1,0:T(8,128)(2,1)} %bitcast.16), calls=%async_computation.3 | async-start | bytes 1835008 | tf_op jit(solution)/shard_map/all_to_all | solution.py:22
  156.1 0.1 convert_reduce_fusion.1
  156.4 31.9 %all-gather = bf16[2048,128]{0,1:T(8,128)(2,1)S(1)} all-gather(bf16[512,128]{0,1:T(8,128)(2,1)S(1)} %fusion.21), channel_id=2, replica_groups=mesh['section'=8,'y'=4,'q'=4,'b'=4] {'b'}, dimensions={0}, use_global_device_ids=true | all-gather | bytes 655360 | tf_op jit(solution)/shard_map/all_gather | solution.py:72
  188.3 0.3 copy.82
  188.5 1.7 fusion.7
  190.2 10.4 %all-to-all-start.4 = ((bf16[64,8,896]{2,1,0:T(8,128)(2,1)}), bf16[64,8,896]{2,1,0:T(8,128)(2,1)S(1)}, u32[]{:S(2)}, u32[]{:S(2)}) async-start(bf16[64,8,896]{2,1,0:T(8,128)(2,1)} %fusion.7), calls=%async_computation.4 | async-start | bytes 1835008 | tf_op jit(solution)/shard_map/all_to_all | solution.py:22
  200.7 44.4 %all-to-all-done.4 = bf16[64,8,896]{2,1,0:T(8,128)(2,1)S(1)} async-done(((bf16[64,8,896]{2,1,0:T(8,128)(2,1)}), bf16[64,8,896]{2,1,0:T(8,128)(2,1)S(1)}, u32[]{:S(2)}, u32[]{:S(2)}) %all-to-all-start.4) | async-done | bytes 917536 | tf_op jit(solution)/shard_map/all_to_all | solution.py:22
  245.1 0.1 convert_reduce_fusion.3
  245.2 0.6 fusion.2
  245.8 1.9 collective-permute-start
  247.8 4.7 %collective-permute-done = bf16[24,3584]{1,0:T(8,128)(2,1)S(1)} collective-permute-done((bf16[24,3584]{1,0:T(8,128)(2,1)S(1)}, bf16[24,3584]{1,0:T(8,128)(2,1)S(1)}, u32[]{:S(2)}, u32[]{:S(2)}) %collective-permute-start) | collective-permute-done | bytes 172064 | tf_op jit(solution)/shard_map/ppermute | solution.py:18
  252.5 0.2 fusion.17
  252.7 0.1 fusion.19
  252.9 0.3 fusion.10
  253.3 54.2 %all_to_all.41 = bf16[64,8,896]{2,1,0:T(8,128)(2,1)S(1)} all-to-all(bf16[64,8,896]{2,1,0:T(8,128)(2,1)S(1)} %bitcast.116), channel_id=1, replica_groups=mesh['section'=8,'y'=4,'q'=4,'b'=4] {'y','q','b'}, dimensions={0} | all-to-all | bytes 1835008 | tf_op jit(solution)/shard_map/all_to_all | solution.py:22
  307.6 1.3 fusion.6
  308.9 25.2 %all_to_all.42 = bf16[4,512,256]{1,2,0:T(8,128)(2,1)S(1)} all-to-all(bf16[4,512,256]{1,2,0:T(8,128)(2,1)S(1)} %fusion.6), channel_id=1, replica_groups=mesh['section'=8,'y'=4,'q'=4,'b'=4] {'b'}, dimensions={0} | all-to-all | bytes 2097152 | tf_op jit(solution)/shard_map/all_to_all | solution.py:22
  334.0 0.1 convert_reduce_fusion
  334.2 15.5 %all-gather.1 = bf16[2048,128]{0,1:T(8,128)(2,1)S(1)} all-gather(bf16[512,128]{0,1:T(8,128)(2,1)S(1)} %fusion.20), channel_id=3, replica_groups=mesh['section'=8,'y'=4,'q'=4,'b'=4] {'b'}, dimensions={0}, use_global_device_ids=true | all-gather | bytes 655360 | tf_op jit(solution)/shard_map/all_gather | solution.py:72
  349.7 0.3 copy.91
  350.0 1.6 fusion.8
  351.6 10.1 %all-to-all-start.7 = ((bf16[64,8,896]{2,1,0:T(8,128)(2,1)}), bf16[64,8,896]{2,1,0:T(8,128)(2,1)S(1)}, u32[]{:S(2)}, u32[]{:S(2)}) async-start(bf16[64,8,896]{2,1,0:T(8,128)(2,1)} %fusion.8), calls=%async_computation.7 | async-start | bytes 1835008 | tf_op jit(solution)/shard_map/all_to_all | solution.py:22
  361.8 45.3 %all-to-all-done.7 = bf16[64,8,896]{2,1,0:T(8,128)(2,1)S(1)} async-done(((bf16[64,8,896]{2,1,0:T(8,128)(2,1)}), bf16[64,8,896]{2,1,0:T(8,128)(2,1)S(1)}, u32[]{:S(2)}, u32[]{:S(2)}) %all-to-all-start.7) | async-done | bytes 917536 | tf_op jit(solution)/shard_map/all_to_all | solution.py:22
  407.1 0.1 convert_reduce_fusion.2
  407.2 1.2 fusion.4
  (41 shorter events, 1.8 us)
Async XLA Ops:
  7.6 19.7 %copy-start.3 = (bf16[1,3584,128]{2,1,0:T(8,128)(2,1)S(1)}, bf16[1,3584,128]{2,1,0:T(8,128)(2,1)}, u32[]{:S(2)}) copy-start(bf16[1,3584,128]{2,1,0:T(8,128)(2,1)} %param.13) | copy-start | bytes 2752516
  8.6 19.3 %copy-start.4 = (bf16[1,3584,128]{2,1,0:T(8,128)(2,1)S(1)}, bf16[1,3584,128]{2,1,0:T(8,128)(2,1)}, u32[]{:S(2)}) copy-start(bf16[1,3584,128]{2,1,0:T(8,128)(2,1)} %param.14) | copy-start | bytes 2752516
  8.6 66.7 %all-to-all-start.1 = ((bf16[64,8,896]{2,1,0:T(8,128)(2,1)}), bf16[64,8,896]{2,1,0:T(8,128)(2,1)}, u32[]{:S(2)}, u32[]{:S(2)}) async-start(bf16[64,8,896]{2,1,0:T(8,128)(2,1)} %bitcast.10), calls=%async_computation.1 | async-start | bytes 1835008 | tf_op jit(solution)/shard_map/all_to_all | solution.py:22
  117.9 1.3 copy-start
  122.7 5.4 %copy-start.5 = (bf16[1,128,3584]{2,1,0:T(8,128)(2,1)S(1)}, bf16[1,128,3584]{2,1,0:T(8,128)(2,1)}, u32[]{:S(2)}) copy-start(bf16[1,128,3584]{2,1,0:T(8,128)(2,1)} %param.15) | copy-start | bytes 2752516
  122.7 26.7 %all-to-all-start.2 = ((bf16[4,512,256]{1,2,0:T(8,128)(2,1)}), bf16[4,512,256]{1,2,0:T(8,128)(2,1)S(1)}, u32[]{:S(2)}, u32[]{:S(2)}) async-start(bf16[4,512,256]{1,2,0:T(8,128)(2,1)} %fusion.5), calls=%async_computation.2 | async-start | bytes 2097152 | tf_op jit(solution)/shard_map/all_to_all | solution.py:22
  149.4 39.1 %all-to-all-start.3 = ((bf16[4,128,896]{2,1,0:T(8,128)(2,1)}), bf16[4,128,896]{2,1,0:T(8,128)(2,1)S(1)}, u32[]{:S(2)}, u32[]{:S(2)}) async-start(bf16[4,128,896]{2,1,0:T(8,128)(2,1)} %bitcast.16), calls=%async_computation.3 | async-start | bytes 1835008 | tf_op jit(solution)/shard_map/all_to_all | solution.py:22
  190.2 55.0 %copy-start.2 = (bf16[1,24,3584]{2,1,0:T(8,128)(2,1)S(1)}, bf16[1,24,3584]{2,1,0:T(8,128)(2,1)}, u32[]{:S(2)}) copy-start(bf16[1,24,3584]{2,1,0:T(8,128)(2,1)} %param.8) | copy-start | bytes 516100
  190.2 54.9 %all-to-all-start.4 = ((bf16[64,8,896]{2,1,0:T(8,128)(2,1)}), bf16[64,8,896]{2,1,0:T(8,128)(2,1)S(1)}, u32[]{:S(2)}, u32[]{:S(2)}) async-start(bf16[64,8,896]{2,1,0:T(8,128)(2,1)} %fusion.7), calls=%async_computation.4 | async-start | bytes 1835008 | tf_op jit(solution)/shard_map/all_to_all | solution.py:22
  200.6 52.0 %copy-start.7 = (bf16[24,3584]{1,0:T(8,128)(2,1)S(1)}, bf16[24,3584]{1,0:T(8,128)(2,1)}, u32[]{:S(2)}) copy-start(bf16[24,3584]{1,0:T(8,128)(2,1)} %param.9) | copy-start | bytes 516100
  245.8 7.5 %copy-start.6 = (bf16[24,3584]{1,0:T(8,128)(2,1)}, bf16[24,3584]{1,0:T(8,128)(2,1)S(1)}, u32[]{:S(2)}) copy-start(bf16[24,3584]{1,0:T(8,128)(2,1)S(1)} %fusion.2) | copy-start | bytes 516100
  245.8 6.7 %collective-permute-start = (bf16[24,3584]{1,0:T(8,128)(2,1)S(1)}, bf16[24,3584]{1,0:T(8,128)(2,1)S(1)}, u32[]{:S(2)}, u32[]{:S(2)}) collective-permute-start(bf16[24,3584]{1,0:T(8,128)(2,1)S(1)} %fusion.2), channel_id=1, source_target_pairs={{0,64},{64,128},{128,192},{192,256},{256,320},{320,384},{384,448},... | collective-permute-start | bytes 516104 | tf_op jit(solution)/shard_map/ppermute | solution.py:18
  253.2 54.3 %copy-start.1 = (bf16[4,896,256]{1,2,0:T(8,128)(2,1)S(1)}, bf16[4,896,256]{1,2,0:T(8,128)(2,1)}, u32[]{:S(2)}) copy-start(bf16[4,896,256]{1,2,0:T(8,128)(2,1)} %copy-done) | copy-start | bytes 5505028
  351.6 55.4 %all-to-all-start.7 = ((bf16[64,8,896]{2,1,0:T(8,128)(2,1)}), bf16[64,8,896]{2,1,0:T(8,128)(2,1)S(1)}, u32[]{:S(2)}, u32[]{:S(2)}) async-start(bf16[64,8,896]{2,1,0:T(8,128)(2,1)} %fusion.8), calls=%async_computation.7 | async-start | bytes 1835008 | tf_op jit(solution)/shard_map/all_to_all | solution.py:22

commit v2 on v1

v2 whole, which is shorter than its diff:
```python
import jax
import jax.numpy as jnp
from jax import lax
from jax.sharding import Mesh, PartitionSpec as P

TOPK = 2
HS = 8
QUARTERS = 4


HIGH = lax.Precision.HIGHEST
RING = ("q", "b")
STORE = ("y",) + RING


def shifted(shard, axis, by):
    peers = lax.axis_size(axis)
    pairs = [(i, i + by) for i in range(peers) if 0 <= i + by < peers]
    return lax.ppermute(shard, axis, pairs)


def fetched(shard, axis, ahead):
    peers = lax.axis_size(axis)
    return lax.ppermute(shard, axis, [((i + ahead) % peers, i) for i in range(peers)])


def swap(blocks, axis):
    return lax.all_to_all(blocks, axis, split_axis=0, concat_axis=0, tiled=True)


def norm_rows(acts, gain):
    values = acts.astype(jnp.float32)
    scale = lax.rsqrt(jnp.mean(values * values, axis=-1, keepdims=True) + 1e-06)
    return ((values * scale * gain).astype(jnp.bfloat16), values)


def row_tables(picks, weights, wanted, capacity):
    blocks, rows, _ = picks.shape
    hit = (picks[None] == wanted[:, None, None, None]).astype(jnp.float32)
    gate = jnp.sum(hit * weights[None], axis=-1)
    hit = jnp.sum(hit, axis=-1)
    earlier = jnp.triu(jnp.ones((rows, rows), jnp.float32), 1)
    position = jnp.einsum("dst,tu->dsu", hit, earlier, precision=HIGH).astype(jnp.int32)
    place = jnp.arange(blocks, dtype=jnp.int32)[None, :, None] * capacity + position
    place = jnp.where(hit > 0, place, -1).reshape(wanted.shape[0], blocks * rows)
    slots = jnp.arange(blocks * capacity, dtype=jnp.int32)
    pack = (slots[None, :, None] == place[:, None, :]).astype(jnp.bfloat16)
    chosen = (place[:, :, None] == slots[None, None, :]).astype(jnp.float32)
    unpack = chosen * gate.reshape(wanted.shape[0], blocks * rows, 1)
    return (pack, unpack)


def layer(acts, tables, gain, in_w, out_w):
    pack, unpack = tables
    rows, width = acts.shape
    part = width // QUARTERS
    normed, values = norm_rows(acts, gain)
    tokens = lax.all_gather(normed, RING, tiled=True)
    packed = []
    for ahead in range(QUARTERS):
        inner = jnp.dot(tokens, in_w[ahead], preferred_element_type=jnp.float32)
        mine = inner.shape[1] // 2
        hidden = (jax.nn.silu(inner[:, :mine]) * inner[:, mine:]).astype(jnp.bfloat16)
        packed.append(
            jnp.dot(pack[ahead], hidden, preferred_element_type=jnp.float32).astype(jnp.bfloat16)
        )
    hidden = lax.all_gather(jnp.stack(packed), "b", axis=0)
    mixed = 0.0
    for ahead in range(QUARTERS):
        units = hidden[:, ahead].transpose(1, 0, 2).reshape(hidden.shape[2], -1)
        out = jnp.dot(units, out_w[ahead], preferred_element_type=jnp.float32)
        mixed = mixed + jnp.dot(unpack[ahead], out, precision=HIGH)
    returned = swap(mixed.astype(jnp.bfloat16).reshape(-1, rows, part), RING)
    returned = returned.reshape(-1, QUARTERS, rows, part).astype(jnp.float32)
    summed = jnp.sum(returned, axis=0).transpose(1, 0, 2).reshape(rows, width)
    return (values + summed).astype(jnp.bfloat16)


def on_device(hidden_in, incoming, routes, gates, norm_gain, w_gate, w_up, w_down):
    section_place = lax.axis_index("section")
    rows, width = incoming.shape
    n_store = lax.axis_size(STORE)
    experts = n_store // HS
    capacity = HS * ((rows * TOPK + experts * HS - 1) // (experts * HS))
    part = width // QUARTERS
    in_w = jnp.concatenate([w_gate[0], w_up[0]], axis=1)
    out_w = w_down[0].reshape(-1, QUARTERS, part).transpose(1, 0, 2)
    out_w = swap(out_w, "b").reshape(-1, part)
    in_w = [in_w] + [fetched(in_w, "y", ahead) for ahead in (1, 2, 3)]
    out_w = [out_w] + [fetched(out_w, "y", ahead) for ahead in (1, 2, 3)]

    ring_place = lax.axis_index(RING)
    per_row = lax.axis_size(RING) // HS
    y_place = (lax.axis_index("y") + jnp.arange(QUARTERS, dtype=jnp.int32)) % QUARTERS
    wanted = y_place * per_row + ring_place // HS
    facts = jnp.stack([routes[:, 0].astype(jnp.float32), gates[:, 0]])
    facts = lax.all_gather(facts.reshape(1, -1), RING, tiled=True)
    facts = facts.reshape(-1, 2, 2, rows, TOPK)
    tables = [
        row_tables(facts[:, 0, t].astype(jnp.int32), facts[:, 1, t], wanted, capacity)
        for t in range(2)
    ]
    first = layer(hidden_in[0], tables[0], norm_gain[0], in_w, out_w)
    handed = shifted(first, "section", 1)
    entry = jnp.where(section_place == 0, incoming, handed)
    second = layer(entry, tables[1], norm_gain[0], in_w, out_w)
    return (first[None], second[None])


def solution(mesh):
    sections, stores = mesh.devices.shape
    fine = Mesh(
        mesh.devices.reshape(sections, 4, stores // (4 * QUARTERS), QUARTERS),
        ("section",) + STORE,
    )
    placed = (
        P("section", STORE, None),
        P(STORE, None),
        P(None, "section", STORE, None),
        P(None, "section", STORE, None),
        P("section", None),
        P("section", None, STORE),
        P("section", None, STORE),
        P("section", STORE, None),
    )
    return jax.shard_map(
        on_device,
        mesh=fine,
        in_specs=placed,
        out_specs=(P("section", STORE, None), P("section", STORE, None)),
        check_vma=False,
    )
```

time: 409 us -> 367 us (0.90)
  the two profiles are of different devices: /device:TPU:34 before, /device:TPU:32 now
where the time goes in v2:
time: 367 us; the launch traced here: 366 us
  waiting for transfers between devices  123 us (34%)
  blocking collectives  118 us (32%)
  matrix products  42.2 us (11%)
  starting transfers between devices  38.7 us (11%)
  local copies, waits for them, and re-layouts  19 us (5%)
  between operations  14.8 us (4%)
  other arithmetic  10.9 us (3%)
    all_gather x2, waiting for transfers between devices, layer(): tokens = lax.all_gather(normed, RING, tiled=True)  89.9 us
    all_to_all x1, blocking collectives, swap(): return lax.all_to_all(blocks, axis, split_axis=0, concat_axis=0, tiled=True)  48 us
    all_gather x1, blocking collectives, on_device(): facts = lax.all_gather(facts.reshape(1, -1), RING, tiled=True)  40.1 us
    all_gather x2, blocking collectives, layer(): hidden = lax.all_gather(jnp.stack(packed), 'b', axis=0)  29.5 us
    all_to_all x2, waiting for transfers between devices, swap(): return lax.all_to_all(blocks, axis, split_axis=0, concat_axis=0, tiled=True)  22.1 us
    ppermute x6, starting transfers between devices, fetched(): lax.ppermute(shard, axis, [((i + ahead) % peers, i) for i in range(peers)])  19.2 us
    all_to_all x2, starting transfers between devices, swap(): return lax.all_to_all(blocks, axis, split_axis=0, concat_axis=0, tiled=True)  18.1 us
    dot_general x8, matrix products, layer(): inner = jnp.dot(tokens, in_w[ahead], preferred_element_type=jnp.float32)  18.1 us
  transfers between devices with their start and end apart: 11, of which 6 were waited for; matrix products, arithmetic and copies ran while one was open for 10% of the time, Pallas kernels for 0%

profile of v2, /device:TPU:32, one launch (start us, length us, event | category | flops | bytes accessed | tf_op | source)
XLA Modules:
  0.0 366.4 jit_solution(4777105997905845928)
XLA Ops:
  7.2 1.1 fusion.19
  9.0 1.7 fusion.21
  10.8 1.6 copy.76
  12.4 1.3 copy.77
  13.7 9.0 %all-to-all-start = ((bf16[4,128,896]{2,1,0:T(8,128)(2,1)}), bf16[4,128,896]{2,1,0:T(8,128)(2,1)S(1)}, u32[]{:S(2)}, u32[]{:S(2)}) async-start(bf16[4,128,896]{2,1,0:T(8,128)(2,1)} %bitcast.22), calls=%async_computation | async-start | bytes 1835008 | tf_op jit(solution)/shard_map/all_to_all | solution.py:28
  22.6 1.5 pad_maximum_fusion
  24.1 1.9 collective-permute-start.2
  26.0 3.4 collective-permute-start.1
  29.5 3.6 collective-permute-start
  33.4 40.1 %all-gather.2 = f32[16,1,192]{2,1,0:T(1,128)S(1)} all-gather(f32[1,1,192]{2,1,0:T(1,128)S(1)} %reshape.146), channel_id=1, replica_groups=mesh['section'=8,'y'=4,'q'=4,'b'=4] {'q','b'}, dimensions={0}, use_global_device_ids=true | all-gather | bytes 13056 | tf_op jit(solution)/shard_map/all_gather | solution.py:97
  76.3 4.9 %collective-permute-start.3 = (bf16[512,896]{1,0:T(8,128)(2,1)S(1)}, bf16[512,896]{1,0:T(8,128)(2,1)}, u32[]{:S(2)}, u32[]{:S(2)}) collective-permute-start(bf16[512,896]{1,0:T(8,128)(2,1)S(1)} %bitcast.206), channel_id=1, source_target_pairs={{16,0},{32,16},{48,32},{0,48},{17,1},{33,17},{49,33},{1,49},{18,2}... | collective-permute-start | bytes 2752520 | tf_op jit(solution)/shard_map/ppermute | solution.py:24
  81.2 2.5 collective-permute-start.4
  83.7 2.9 collective-permute-start.5
  86.6 8.8 %all-gather.6.cloned.1.call-done = bf16[384,3584]{1,0:T(8,128)(2,1)} async-done(((bf16[24,3584]{1,0:T(8,128)(2,1)}), bf16[384,3584]{1,0:T(8,128)(2,1)}) %all-gather.6.cloned.1.call-update) | async-done | bytes 2752528 | tf_op jit(solution)/shard_map/all_gather | solution.py:58
  95.4 3.3 fusion.80
  100.1 8.1 %collective-permute-done.1 = bf16[3584,256]{1,0:T(8,128)(2,1)} collective-permute-done((bf16[3584,256]{1,0:T(8,128)(2,1)}, bf16[3584,256]{1,0:T(8,128)(2,1)}, u32[]{:S(2)}, u32[]{:S(2)}) %collective-permute-start.1) | collective-permute-done | bytes 1835040 | tf_op jit(solution)/shard_map/ppermute | solution.py:24
  108.2 2.4 fusion.79
  110.6 2.1 collective-permute-done
  112.6 2.4 fusion.78
  115.7 16.0 %all-gather = bf16[16,128,128]{2,1,0:T(8,128)(2,1)S(1)} all-gather(bf16[4,128,128]{2,1,0:T(8,128)(2,1)S(1)} %pad_maximum_fusion.1), channel_id=2, replica_groups=mesh['section'=8,'y'=4,'q'=4,'b'=4] {'b'}, dimensions={0}, use_global_device_ids=true | all-gather | bytes 655360 | tf_op jit(solution)/shard_map/all_gather | solution.py:67
  133.3 1.7 copy.78
  135.0 1.7 copy.79
  136.6 2.4 fusion.81
  139.0 2.0 fusion.82
  141.0 2.0 convolution_bitcast_fusion.1
  143.0 1.7 copy.80
  144.7 2.3 fusion.37
  147.0 1.2 convolution_add_fusion.5
  148.3 1.2 convolution_add_fusion.4
  149.9 1.2 fusion
  151.2 48.0 %all_to_all.15 = bf16[16,24,896]{2,1,0:T(8,128)(2,1)S(1)} all-to-all(bf16[16,24,896]{2,1,0:T(8,128)(2,1)S(1)} %bitcast.213), channel_id=1, replica_groups=mesh['section'=8,'y'=4,'q'=4,'b'=4] {'q','b'}, dimensions={0} | all-to-all | bytes 1376256 | tf_op jit(solution)/shard_map/all_to_all | solution.py:28
  200.1 1.3 collective-permute-start.6
  205.8 81.0 %all-gather.8.cloned.1.call-done = bf16[384,3584]{1,0:T(8,128)(2,1)} async-done(((bf16[24,3584]{1,0:T(8,128)(2,1)}), bf16[384,3584]{1,0:T(8,128)(2,1)}) %all-gather.8.cloned.1.call-update) | async-done | bytes 2752528 | tf_op jit(solution)/shard_map/all_gather | solution.py:58
  286.8 3.3 fusion.86
  290.4 2.4 fusion.85
  293.1 2.5 fusion.84
  297.0 13.6 %all-gather.1 = bf16[16,128,128]{2,1,0:T(8,128)(2,1)S(1)} all-gather(bf16[4,128,128]{2,1,0:T(8,128)(2,1)S(1)} %pad_maximum_fusion.2), channel_id=3, replica_groups=mesh['section'=8,'y'=4,'q'=4,'b'=4] {'b'}, dimensions={0}, use_global_device_ids=true | all-gather | bytes 655360 | tf_op jit(solution)/shard_map/all_gather | solution.py:67
  312.1 1.7 copy.86
  313.7 1.7 copy.87
  315.4 1.7 copy.88
  317.1 1.2 convolution_bitcast_fusion
  318.3 1.2 fusion.32
  319.6 1.5 fusion.87
  321.1 1.2 convolution_add_fusion.2
  322.7 1.2 convolution_add_fusion.1
  324.3 2.1 fusion.1
  326.4 9.2 %all-to-all-start.2 = ((bf16[16,24,896]{2,1,0:T(8,128)(2,1)}), bf16[16,24,896]{2,1,0:T(8,128)(2,1)S(1)}, u32[]{:S(2)}, u32[]{:S(2)}) async-start(bf16[16,24,896]{2,1,0:T(8,128)(2,1)} %bitcast.67), calls=%async_computation.2 | async-start | bytes 1376256 | tf_op jit(solution)/shard_map/all_to_all | solution.py:28
  336.6 22.1 %all-to-all-done.2 = bf16[16,24,896]{2,1,0:T(8,128)(2,1)S(1)} async-done(((bf16[16,24,896]{2,1,0:T(8,128)(2,1)}), bf16[16,24,896]{2,1,0:T(8,128)(2,1)S(1)}, u32[]{:S(2)}, u32[]{:S(2)}) %all-to-all-start.2) | async-done | bytes 688160 | tf_op jit(solution)/shard_map/all_to_all | solution.py:28
  (126 shorter events, 18.8 us)
Async XLA Ops:
  7.2 88.3 %all-gather.6.cloned.1.call-start = ((), (), s32[]{:S(2)}) async-start(), calls=%async_computation.3 | async-start | bytes 2924544 | tf_op jit(solution)/shard_map/all_gather | solution.py:58
  12.3 10.3 %copy-start.10 = (bf16[1,3584,128]{2,1,0:T(8,128)(2,1)S(1)}, bf16[1,3584,128]{2,1,0:T(8,128)(2,1)}, u32[]{:S(2)}) copy-start(bf16[1,3584,128]{2,1,0:T(8,128)(2,1)} %param.14) | copy-start | bytes 2752516
  12.3 10.3 %copy-start.13 = (bf16[1,3584,128]{2,1,0:T(8,128)(2,1)S(1)}, bf16[1,3584,128]{2,1,0:T(8,128)(2,1)}, u32[]{:S(2)}) copy-start(bf16[1,3584,128]{2,1,0:T(8,128)(2,1)} %param.13) | copy-start | bytes 2752516
  13.7 62.6 %all-to-all-start = ((bf16[4,128,896]{2,1,0:T(8,128)(2,1)}), bf16[4,128,896]{2,1,0:T(8,128)(2,1)S(1)}, u32[]{:S(2)}, u32[]{:S(2)}) async-start(bf16[4,128,896]{2,1,0:T(8,128)(2,1)} %bitcast.22), calls=%async_computation | async-start | bytes 1835008 | tf_op jit(solution)/shard_map/all_to_all | solution.py:28
  22.6 264.2 %all-gather.8.cloned.1.call-start = ((), (), s32[]{:S(2)}) async-start(), calls=%async_computation.4 | async-start | bytes 2924544 | tf_op jit(solution)/shard_map/all_gather | solution.py:58
  22.6 10.5 %copy-start.27 = (s32[2,1,24,2]{2,3,1,0:T(2,128)S(1)}, s32[2,1,24,2]{2,3,1,0:T(2,128)}, u32[]{:S(2)}) copy-start(s32[2,1,24,2]{2,3,1,0:T(2,128)} %param.10) | copy-start | bytes 1156
  22.6 10.5 %copy-start.28 = (f32[2,1,24,2]{2,3,1,0:T(2,128)S(1)}, f32[2,1,24,2]{2,3,1,0:T(2,128)}, u32[]{:S(2)}) copy-start(f32[2,1,24,2]{2,3,1,0:T(2,128)} %param.11) | copy-start | bytes 1156
  24.1 59.6 %collective-permute-start.2 = (bf16[3584,256]{1,0:T(8,128)(2,1)}, bf16[3584,256]{1,0:T(8,128)(2,1)}, u32[]{:S(2)}, u32[]{:S(2)}) collective-permute-start(bf16[3584,256]{1,0:T(8,128)(2,1)} %pad_maximum_fusion), channel_id=1, source_target_pairs={{48,0},{0,16},{16,32},{32,48},{49,1},{1,17},{17,33},{33,49},{50,2}... | collective-permute-start | bytes 5505032 | tf_op jit(solution)/shard_map/ppermute | solution.py:24
  26.0 82.2 %collective-permute-start.1 = (bf16[3584,256]{1,0:T(8,128)(2,1)}, bf16[3584,256]{1,0:T(8,128)(2,1)}, u32[]{:S(2)}, u32[]{:S(2)}) collective-permute-start(bf16[3584,256]{1,0:T(8,128)(2,1)} %pad_maximum_fusion), channel_id=1, source_target_pairs={{32,0},{48,16},{0,32},{16,48},{33,1},{49,17},{1,33},{17,49},{34,2}... | collective-permute-start | bytes 5505032 | tf_op jit(solution)/shard_map/ppermute | solution.py:24
  29.5 83.2 %collective-permute-start = (bf16[3584,256]{1,0:T(8,128)(2,1)}, bf16[3584,256]{1,0:T(8,128)(2,1)}, u32[]{:S(2)}, u32[]{:S(2)}) collective-permute-start(bf16[3584,256]{1,0:T(8,128)(2,1)} %pad_maximum_fusion), channel_id=1, source_target_pairs={{16,0},{32,16},{48,32},{0,48},{17,1},{33,17},{49,33},{1,49},{18,2}... | collective-permute-start | bytes 5505032 | tf_op jit(solution)/shard_map/ppermute | solution.py:24
  73.6 10.1 %copy-start.25 = (s32[16]{0:T(128)}, s32[16]{0:T(128)S(1)}, u32[]{:S(2)}) copy-start(s32[16]{0:T(128)S(1)} %iota_multiply_fusion) | copy-start | bytes 196
  76.3 60.3 %collective-permute-start.3 = (bf16[512,896]{1,0:T(8,128)(2,1)S(1)}, bf16[512,896]{1,0:T(8,128)(2,1)}, u32[]{:S(2)}, u32[]{:S(2)}) collective-permute-start(bf16[512,896]{1,0:T(8,128)(2,1)S(1)} %bitcast.206), channel_id=1, source_target_pairs={{16,0},{32,16},{48,32},{0,48},{17,1},{33,17},{49,33},{1,49},{18,2}... | collective-permute-start | bytes 2752520 | tf_op jit(solution)/shard_map/ppermute | solution.py:24
  81.2 57.9 %collective-permute-start.4 = (bf16[512,896]{1,0:T(8,128)(2,1)S(1)}, bf16[512,896]{1,0:T(8,128)(2,1)S(1)}, u32[]{:S(2)}, u32[]{:S(2)}) collective-permute-start(bf16[512,896]{1,0:T(8,128)(2,1)S(1)} %bitcast.207), channel_id=1, source_target_pairs={{32,0},{48,16},{0,32},{16,48},{33,1},{49,17},{1,33},{17,49},{34,2}... | collective-permute-start | bytes 2752520 | tf_op jit(solution)/shard_map/ppermute | solution.py:24
  83.7 65.8 %collective-permute-start.5 = (bf16[512,896]{1,0:T(8,128)(2,1)S(1)}, bf16[512,896]{1,0:T(8,128)(2,1)S(1)}, u32[]{:S(2)}, u32[]{:S(2)}) collective-permute-start(bf16[512,896]{1,0:T(8,128)(2,1)S(1)} %bitcast.208), channel_id=1, source_target_pairs={{48,0},{0,16},{16,32},{32,48},{49,1},{1,17},{17,33},{33,49},{50,2}... | collective-permute-start | bytes 2752520 | tf_op jit(solution)/shard_map/ppermute | solution.py:24
  95.4 3.4 copy-start.20
  95.4 3.6 copy-start.11
  95.4 3.6 copy-start.14
  95.4 3.8 %copy-start.29 = (bf16[384,3584]{1,0:T(8,128)(2,1)S(1)}, bf16[384,3584]{1,0:T(8,128)(2,1)}, u32[]{:S(2)}) copy-start(bf16[384,3584]{1,0:T(8,128)(2,1)} %all-gather.6.cloned.1.call-done) | copy-start | bytes 8257540
  131.7 0.8 copy-start.4
  144.7 2.3 copy-start.6
  147.0 1.3 copy-start.7
  148.3 1.3 copy-start.18
  151.1 48.9 %copy-start.2 = (bf16[1,24,3584]{2,1,0:T(8,128)(2,1)S(1)}, bf16[1,24,3584]{2,1,0:T(8,128)(2,1)}, u32[]{:S(2)}) copy-start(bf16[1,24,3584]{2,1,0:T(8,128)(2,1)} %param.8) | copy-start | bytes 516100
  151.2 51.3 %copy-start.22 = (bf16[24,3584]{1,0:T(8,128)(2,1)S(1)}, bf16[24,3584]{1,0:T(8,128)(2,1)}, u32[]{:S(2)}) copy-start(bf16[24,3584]{1,0:T(8,128)(2,1)} %param.9) | copy-start | bytes 516100
  199.2 4.9 %copy-start.24 = (f32[4,16,24]{2,1,0:T(8,128)S(1)}, f32[4,16,24]{2,1,0:T(8,128)}, u32[]{:S(2)}) copy-start(f32[4,16,24]{2,1,0:T(8,128)} %get-tuple-element.3) | copy-start | bytes 18436
  199.2 4.9 %copy-start.26 = (s32[16]{0:T(128)S(1)}, s32[16]{0:T(128)}, u32[]{:S(2)}) copy-start(s32[16]{0:T(128)} %copy-done.25) | copy-start | bytes 196
  199.2 5.2 %copy-start.23 = (f32[4,16,24]{2,1,0:T(8,128)S(1)}, f32[4,16,24]{2,1,0:T(8,128)}, u32[]{:S(2)}) copy-start(f32[4,16,24]{2,1,0:T(8,128)} %get-tuple-element.2) | copy-start | bytes 18436
  199.3 0.8 copy-start
  200.1 2.3 collective-permute-start.6
  202.6 0.7 copy-start.8
  286.8 3.4 copy-start.21
  286.8 3.6 copy-start.30
  293.0 2.8 copy-start.12
  293.0 2.8 copy-start.15
  310.5 0.8 copy-start.5
  317.1 2.5 copy-start.19
  321.1 1.3 copy-start.17
  322.7 1.3 copy-start.16
  324.3 11.3 %copy-start.1 = (f32[4,24,896]{2,1,0:T(8,128)S(1)}, f32[4,24,896]{2,1,0:T(8,128)}, u32[]{:S(2)}) copy-start(f32[4,24,896]{2,1,0:T(8,128)} %copy-done) | copy-start | bytes 1032196
  326.4 9.4 %copy-start.3 = (bf16[1,24,3584]{2,1,0:T(8,128)(2,1)S(1)}, bf16[1,24,3584]{2,1,0:T(8,128)(2,1)}, u32[]{:S(2)}) copy-start(bf16[1,24,3584]{2,1,0:T(8,128)(2,1)} %param.8) | copy-start | bytes 516100
  326.4 32.3 %all-to-all-start.2 = ((bf16[16,24,896]{2,1,0:T(8,128)(2,1)}), bf16[16,24,896]{2,1,0:T(8,128)(2,1)S(1)}, u32[]{:S(2)}, u32[]{:S(2)}) async-start(bf16[16,24,896]{2,1,0:T(8,128)(2,1)} %bitcast.67), calls=%async_computation.2 | async-start | bytes 1376256 | tf_op jit(solution)/shard_map/all_to_all | solution.py:28
  335.6 23.2 %copy-start.9 = (bf16[24,3584]{1,0:T(8,128)(2,1)S(1)}, bf16[24,3584]{1,0:T(8,128)(2,1)}, u32[]{:S(2)}) copy-start(bf16[24,3584]{1,0:T(8,128)(2,1)} %copy-done.8) | copy-start | bytes 516100
Sparse Core Ops, SparseCore 0:
  10.9 84.5 all-gather.5
  204.2 82.5 all-gather.7

commit v3 on v2

v3 whole, which is shorter than its diff:
```python
import functools

import jax
import jax.numpy as jnp
from jax import lax
from jax.experimental import pallas as pl
from jax.experimental.pallas import tpu as pltpu
from jax.sharding import Mesh, PartitionSpec as P

TOPK = 2
HS = 8
QUARTERS = 4


HIGH = lax.Precision.HIGHEST
RING = ("q", "b")
STORE = ("y",) + RING
MIB = 1 << 20


def shifted(shard, axis, by):
    peers = lax.axis_size(axis)
    pairs = [(i, i + by) for i in range(peers) if 0 <= i + by < peers]
    return lax.ppermute(shard, axis, pairs)


def fetched(shard, axis, ahead):
    peers = lax.axis_size(axis)
    return lax.ppermute(shard, axis, [((i + ahead) % peers, i) for i in range(peers)])


def swap(blocks, axis):
    return lax.all_to_all(blocks, axis, split_axis=0, concat_axis=0, tiled=True)


def whole_row(shard):
    half = shard.shape[0] // 2
    after = fetched(shard, "y", 1)
    before = fetched(shard, "y", 3)
    far_top = fetched(after[:half], "y", 1)
    far_bottom = fetched(before[half:], "y", 3)
    return (shard, after, far_top, far_bottom, before)


def loads(pieces, buffer, sems):
    own, after, far_top, far_bottom, before = pieces
    half = far_top.shape[0]
    return [
        [pltpu.make_async_copy(own, buffer.at[0], sems.at[0])],
        [pltpu.make_async_copy(after, buffer.at[1], sems.at[1])],
        [
            pltpu.make_async_copy(far_top, buffer.at[2, pl.ds(0, half)], sems.at[2]),
            pltpu.make_async_copy(far_bottom, buffer.at[2, pl.ds(half, half)], sems.at[3]),
        ],
        [pltpu.make_async_copy(before, buffer.at[3], sems.at[4])],
    ]


def entry_kernel(first_ref, fed_ref, handed_ref, gain_ref, entry_ref, normed_ref):
    acts = jnp.where(first_ref[0] == 1, fed_ref[...], handed_ref[...])
    entry_ref[...] = acts
    values = acts.astype(jnp.float32)
    scale = lax.rsqrt(jnp.mean(values * values, axis=-1, keepdims=True) + 1e-06)
    normed_ref[...] = (values * scale * gain_ref[...]).astype(jnp.bfloat16)


def enter(is_first, fed, handed, gain):
    vmem = pl.BlockSpec(memory_space=pltpu.VMEM)
    return pl.pallas_call(
        entry_kernel,
        out_shape=(jax.ShapeDtypeStruct(fed.shape, fed.dtype),) * 2,
        in_specs=[pl.BlockSpec(memory_space=pltpu.SMEM), vmem, vmem, vmem],
        out_specs=(vmem, vmem),
        cost_estimate=pl.CostEstimate(flops=6 * fed.size, bytes_accessed=8 * fed.size, transcendentals=0),
        name="enter",
    )(is_first, fed, handed, gain)


def up_kernel(tokens_ref, own, after, far_top, far_bottom, before, place_ref, packed_ref, tokens, weights, sems, token_sem):
    token_copy = pltpu.make_async_copy(tokens_ref, tokens, token_sem)
    token_copy.start()
    copies = loads((own, after, far_top, far_bottom, before), weights, sems)
    for group in copies:
        for copy in group:
            copy.start()
    token_copy.wait()
    rows = tokens.shape[0]
    slots = packed_ref.shape[1]
    for ahead in range(QUARTERS):
        for copy in copies[ahead]:
            copy.wait()
        inner = jnp.dot(tokens[...], weights[ahead], preferred_element_type=jnp.float32)
        mine = inner.shape[1] // 2
        gate = inner[:, :mine]
        hidden = (gate / (1.0 + jnp.exp(-gate)) * inner[:, mine:]).astype(jnp.bfloat16)
        slot = lax.broadcasted_iota(jnp.int32, (slots, rows), 0)
        pack = jnp.where(slot == place_ref[ahead : ahead + 1, :], 1.0, 0.0).astype(jnp.bfloat16)
        packed = jnp.dot(pack, hidden, preferred_element_type=jnp.float32)
        packed_ref[ahead] = packed.astype(jnp.bfloat16)


def expert_up(tokens, in_w, place, slots):
    rows, width = tokens.shape
    units = in_w[0].shape[1]
    any_space = pl.BlockSpec(memory_space=pl.ANY)
    vmem = pl.BlockSpec(memory_space=pltpu.VMEM)
    return pl.pallas_call(
        up_kernel,
        out_shape=jax.ShapeDtypeStruct((QUARTERS, slots, units // 2), jnp.bfloat16),
        in_specs=[any_space] * 6 + [vmem],
        out_specs=vmem,
        scratch_shapes=[
            pltpu.VMEM((rows, width), jnp.bfloat16),
            pltpu.VMEM((QUARTERS, width, units), jnp.bfloat16),
            pltpu.SemaphoreType.DMA((5,)),
            pltpu.SemaphoreType.DMA,
        ],
        compiler_params=pltpu.CompilerParams(vmem_limit_bytes=32 * MIB),
        cost_estimate=pl.CostEstimate(
            flops=2 * QUARTERS * rows * width * units,
            bytes_accessed=2 * width * (rows + QUARTERS * units),
            transcendentals=rows * units * 2,
        ),
        name="expert_up",
    )(tokens, *in_w, place)


def down_kernel(hidden_ref, own, after, far_top, far_bottom, before, place_ref, gate_ref, out_ref, weights, sems):
    copies = loads((own, after, far_top, far_bottom, before), weights, sems)
    for group in copies:
        for copy in group:
            copy.start()
    rows = out_ref.shape[0]
    slots = hidden_ref.shape[2]
    mixed = None
    for ahead in range(QUARTERS):
        for copy in copies[ahead]:
            copy.wait()
        units = jnp.concatenate([hidden_ref[b, ahead] for b in range(QUARTERS)], axis=1)
        out = jnp.dot(units, weights[ahead], preferred_element_type=jnp.float32)
        high = out.astype(jnp.bfloat16)
        low = (out - high.astype(jnp.float32)).astype(jnp.bfloat16)
        slot = lax.broadcasted_iota(jnp.int32, (rows, slots), 1)
        unpack = jnp.where(slot == place_ref[:, ahead : ahead + 1], 1.0, 0.0).astype(jnp.bfloat16)
        placed = jnp.dot(unpack, high, preferred_element_type=jnp.float32)
        placed = placed + jnp.dot(unpack, low, preferred_element_type=jnp.float32)
        placed = placed * gate_ref[:, ahead : ahead + 1]
        mixed = placed if mixed is None else mixed + placed
    out_ref[...] = mixed.astype(jnp.bfloat16)


def expert_down(hidden, out_w, place, gate):
    rows = place.shape[0]
    units, part = out_w[0].shape
    slots = hidden.shape[2]
    any_space = pl.BlockSpec(memory_space=pl.ANY)
    vmem = pl.BlockSpec(memory_space=pltpu.VMEM)
    return pl.pallas_call(
        down_kernel,
        out_shape=jax.ShapeDtypeStruct((rows, part), jnp.bfloat16),
        in_specs=[vmem] + [any_space] * 5 + [vmem] * 2,
        out_specs=vmem,
        scratch_shapes=[
            pltpu.VMEM((QUARTERS, units, part), jnp.bfloat16),
            pltpu.SemaphoreType.DMA((5,)),
        ],
        compiler_params=pltpu.CompilerParams(vmem_limit_bytes=32 * MIB),
        cost_estimate=pl.CostEstimate(
            flops=2 * QUARTERS * slots * part * (units + 2 * rows),
            bytes_accessed=2 * QUARTERS * units * (part + slots),
            transcendentals=0,
        ),
        name="expert_down",
    )(hidden, *out_w, place, gate)


def leave_kernel(entry_ref, returned_ref, out_ref):
    part = returned_ref.shape[2]
    for b in range(QUARTERS):
        columns = pl.ds(b * part, part)
        total = entry_ref[:, columns].astype(jnp.float32)
        for q in range(returned_ref.shape[0] // QUARTERS):
            total = total + returned_ref[q * QUARTERS + b].astype(jnp.float32)
        out_ref[:, columns] = total.astype(jnp.bfloat16)


def leave(entry, returned):
    vmem = pl.BlockSpec(memory_space=pltpu.VMEM)
    return pl.pallas_call(
        leave_kernel,
        out_shape=jax.ShapeDtypeStruct(entry.shape, jnp.bfloat16),
        in_specs=[vmem] * 2,
        out_specs=vmem,
        cost_estimate=pl.CostEstimate(
            flops=returned.size, bytes_accessed=2 * returned.size + 4 * entry.size, transcendentals=0
        ),
        name="leave",
    )(entry, returned)


def row_tables(picks, weights, wanted, capacity):
    blocks, rows, _ = picks.shape
    hit = (picks[None] == wanted[:, None, None, None]).astype(jnp.float32)
    gate = jnp.sum(hit * weights[None], axis=-1)
    hit = jnp.sum(hit, axis=-1)
    earlier = jnp.triu(jnp.ones((rows, rows), jnp.float32), 1)
    position = jnp.einsum("dst,tu->dsu", hit, earlier, precision=HIGH).astype(jnp.int32)
    place = jnp.arange(blocks, dtype=jnp.int32)[None, :, None] * capacity + position
    place = jnp.where(hit > 0, place, -1).reshape(wanted.shape[0], blocks * rows)
    return (place, place.T, gate.reshape(wanted.shape[0], blocks * rows).T)


def layer(entry, normed, tables, in_w, out_w, slots):
    place, place_t, gate_t = tables
    rows, width = entry.shape
    tokens = lax.all_gather(normed, RING, tiled=True)
    hidden = expert_up(tokens, in_w, place, slots)
    hidden = lax.all_gather(hidden, "b", axis=0)
    mixed = expert_down(hidden, out_w, place_t, gate_t)
    returned = swap(mixed.reshape(-1, rows, width // QUARTERS), RING)
    return leave(entry, returned)


def on_device(hidden_in, incoming, routes, gates, norm_gain, w_gate, w_up, w_down):
    section_place = lax.axis_index("section")
    rows, width = incoming.shape
    n_store = lax.axis_size(STORE)
    experts = n_store // HS
    capacity = HS * ((rows * TOPK + experts * HS - 1) // (experts * HS))
    part = width // QUARTERS
    one = jnp.ones((1,), jnp.int32)
    entry, normed = enter(one, hidden_in[0], hidden_in[0], norm_gain)

    in_w = whole_row(jnp.concatenate([w_gate[0], w_up[0]], axis=1))
    out_w = w_down[0].reshape(-1, QUARTERS, part).transpose(1, 0, 2)
    out_w = whole_row(swap(out_w, "b").reshape(-1, part))

    ring = lax.axis_size(RING)
    ring_place = lax.axis_index(RING)
    y_place = (lax.axis_index("y") + jnp.arange(QUARTERS, dtype=jnp.int32)) % QUARTERS
    wanted = y_place * (ring // HS) + ring_place // HS
    facts = jnp.stack([routes[:, 0].astype(jnp.float32), gates[:, 0]])
    facts = swap(jnp.broadcast_to(facts.reshape(1, 1, -1), (ring, 1, facts.size)), RING)
    facts = facts.reshape(ring, 2, 2, rows, TOPK)
    tables = [
        row_tables(facts[:, 0, t].astype(jnp.int32), facts[:, 1, t], wanted, capacity)
        for t in range(2)
    ]
    slots = ring * capacity
    first = layer(entry, normed, tables[0], in_w, out_w, slots)
    handed = shifted(first, "section", 1)
    is_first = (section_place == 0).astype(jnp.int32).reshape(1)
    entry, normed = enter(is_first, incoming, handed, norm_gain)
    second = layer(entry, normed, tables[1], in_w, out_w, slots)
    return (first[None], second[None])


def solution(mesh):
    sections, stores = mesh.devices.shape
    fine = Mesh(
        mesh.devices.reshape(sections, 4, stores // (4 * QUARTERS), QUARTERS),
        ("section",) + STORE,
    )
    placed = (
        P("section", STORE, None),
        P(STORE, None),
        P(None, "section", STORE, None),
        P(None, "section", STORE, None),
        P("section", None),
        P("section", None, STORE),
        P("section", None, STORE),
        P("section", STORE, None),
    )
    return jax.shard_map(
        on_device,
        mesh=fine,
        in_specs=placed,
        out_specs=(P("section", STORE, None), P("section", STORE, None)),
        check_vma=False,
    )
```

time: 367 us -> 355 us (0.967)
  matrix products: 42.2 us -> 0.32 us
  Pallas kernels: 0 us -> 31.1 us
  starting transfers between devices: 38.7 us -> 51.6 us
  other arithmetic: 10.9 us -> 0.35 us
  blocking collectives: 118 us -> 112 us
  local copies, waits for them, and re-layouts: 19 us -> 24.7 us
  waiting for transfers between devices: 123 us -> 119 us
    dot_general x32 -> x0, matrix products: 41.9 us -> none  [the longest x8 18.1 us: layer(): inner = jnp.dot(tokens, in_w[ahead], preferred_element_type=jnp.float32)]
    all_gather x3 -> x2, blocking collectives: 69.6 us -> 28.4 us  [layer(): hidden = lax.all_gather(hidden, 'b', axis=0)]
    all_to_all x1 -> x2, blocking collectives: 48 us -> 83.9 us  [swap(): return lax.all_to_all(blocks, axis, split_axis=0, concat_axis=0, tiled=True)]
    pallas_call x0 -> x8, Pallas kernels: none -> 31.1 us  [the longest x2 15.3 us: expert_up(): pl.pallas_call(up_kernel, out_shape=jax.ShapeDtypeStruct((QUARTERS, slots...]
    ppermute x6 -> x8, waiting for transfers between devices: 10.1 us -> 35.6 us  [fetched(): lax.ppermute(shard, axis, [((i + ahead) % peers, i) for i in range(peers)])]
    all_gather x2, waiting for transfers between devices: 89.9 us -> 71.5 us  [layer(): tokens = lax.all_gather(normed, RING, tiled=True)]
    transpose x9 -> x0, local copies, waits for them, and re-layouts: 11.6 us -> none  [the longest x8 11.5 us: layer(): units = hidden[:, ahead].transpose(1, 0, 2).reshape(hidden.shape[2], -1)]
    all_to_all x2, waiting for transfers between devices: 22.1 us -> 11.1 us  [swap(): return lax.all_to_all(blocks, axis, split_axis=0, concat_axis=0, tiled=True)]
  transfers between devices with their start and end apart: 11 -> 13, of which waited for: 6 -> 5; matrix products, arithmetic and copies ran while one was open for 10% -> 3% of each run, Pallas kernels for 0% -> 2%
where the time goes in v3:
time: 355 us; the launch traced here: 354 us
  waiting for transfers between devices  119 us (34%)
  blocking collectives  112 us (32%)
  starting transfers between devices  51.6 us (15%)
  Pallas kernels  31.1 us (9%)
  local copies, waits for them, and re-layouts  24.7 us (7%)
  between operations  14.4 us (4%)
    all_to_all x2, blocking collectives, swap(): return lax.all_to_all(blocks, axis, split_axis=0, concat_axis=0, tiled=True)  83.9 us
    all_gather x2, waiting for transfers between devices, layer(): tokens = lax.all_gather(normed, RING, tiled=True)  71.5 us
    ppermute x8, waiting for transfers between devices, fetched(): lax.ppermute(shard, axis, [((i + ahead) % peers, i) for i in range(peers)])  35.6 us
    all_gather x2, blocking collectives, layer(): hidden = lax.all_gather(hidden, 'b', axis=0)  28.4 us
    ppermute x8, starting transfers between devices, fetched(): lax.ppermute(shard, axis, [((i + ahead) % peers, i) for i in range(peers)])  27.6 us
    all_to_all x2, starting transfers between devices, swap(): return lax.all_to_all(blocks, axis, split_axis=0, concat_axis=0, tiled=True)  22.5 us
    pallas_call x2, Pallas kernels, expert_up(): pl.pallas_call(up_kernel, out_shape=jax.ShapeDtypeStruct((QUARTERS, slots...  15.3 us
    unnamed x36, local copies, waits for them, and re-layouts  14.5 us
  transfers between devices with their start and end apart: 13, of which 5 were waited for; matrix products, arithmetic and copies ran while one was open for 3% of the time, Pallas kernels for 2%

profile of v3, /device:TPU:32, one launch (start us, length us, event | category | flops | bytes accessed | tf_op | source)
XLA Modules:
  0.0 354.0 jit_solution(985437833600466632)
XLA Ops:
  7.2 1.8 enter.2
  9.1 1.9 reshape_squeeze.3
  11.0 1.1 copy.50
  12.1 9.0 %all-to-all-start.1 = ((bf16[4,128,896]{2,1,0:T(8,128)(2,1)}), bf16[4,128,896]{2,1,0:T(8,128)(2,1)S(1)}, u32[]{:S(2)}, u32[]{:S(2)}) async-start(bf16[4,128,896]{2,1,0:T(8,128)(2,1)} %bitcast.46), calls=%async_computation.1 | async-start | bytes 1835008 | tf_op jit(solution)/shard_map/all_to_all | solution.py:33
  21.1 0.2 pad_maximum_fusion.own
  21.3 2.1 collective-permute-start
  23.4 3.9 %collective-permute-start.2 = (bf16[3584,256]{1,0:T(8,128)(2,1)S(1)}, bf16[3584,256]{1,0:T(8,128)(2,1)S(1)}, u32[]{:S(2)}, u32[]{:S(2)}) collective-permute-start(bf16[3584,256]{1,0:T(8,128)(2,1)S(1)} %pad_maximum_fusion.own), channel_id=1, source_target_pairs={{48,0},{0,16},{16,32},{32,48},{49,1},{1,17},{17,33},{33,49},{50,2}... | collective-permute-start | bytes 5505032 | tf_op jit(solution)/shard_map/ppermute | solution.py:29
  27.3 34.8 %collective-permute-done.after = bf16[3584,256]{1,0:T(8,128)(2,1)S(1)} collective-permute-done((bf16[3584,256]{1,0:T(8,128)(2,1)S(1)}, bf16[3584,256]{1,0:T(8,128)(2,1)S(1)}, u32[]{:S(2)}, u32[]{:S(2)}) %collective-permute-start) | collective-permute-done | bytes 1835040 | tf_op jit(solution)/shard_map/ppermute | solution.py:29
  62.1 1.1 slice.32
  63.2 5.6 %collective-permute-start.1 = (bf16[1792,256]{1,0:T(8,128)(2,1)}, bf16[1792,256]{1,0:T(8,128)(2,1)}, u32[]{:S(2)}, u32[]{:S(2)}) collective-permute-start(bf16[1792,256]{1,0:T(8,128)(2,1)} %slice.32), channel_id=1, source_target_pairs={{16,0},{32,16},{48,32},{0,48},{17,1},{33,17},{49,33},{1,49},{18,2}... | collective-permute-start | bytes 2752520 | tf_op jit(solution)/shard_map/ppermute | solution.py:29
  68.8 1.0 slice.33
  69.7 1.3 copy-done.8
  71.0 1.9 collective-permute-start.3
  73.0 5.1 %collective-permute-start.4 = (bf16[512,896]{1,0:T(8,128)(2,1)S(1)}, bf16[512,896]{1,0:T(8,128)(2,1)S(1)}, u32[]{:S(2)}, u32[]{:S(2)}) collective-permute-start(bf16[512,896]{1,0:T(8,128)(2,1)S(1)} %bitcast.47), channel_id=1, source_target_pairs={{16,0},{32,16},{48,32},{0,48},{17,1},{33,17},{49,33},{1,49},{18,2}... | collective-permute-start | bytes 2752520 | tf_op jit(solution)/shard_map/ppermute | solution.py:29
  78.1 1.9 collective-permute-start.6
  80.3 0.6 broadcast_in_dim.30
  80.9 13.5 %all-to-all-start = ((f32[16,1,192]{2,1,0:T(1,128)}), f32[16,1,192]{2,1,0:T(1,128)S(1)}, u32[]{:S(2)}, u32[]{:S(2)}) async-start(f32[16,1,192]{2,1,0:T(1,128)} %broadcast_in_dim.30), calls=%async_computation | async-start | bytes 32768 | tf_op jit(solution)/shard_map/all_to_all | solution.py:33
  94.5 11.1 %all-to-all-done = f32[16,1,192]{2,1,0:T(1,128)S(1)} async-done(((f32[16,1,192]{2,1,0:T(1,128)}), f32[16,1,192]{2,1,0:T(1,128)S(1)}, u32[]{:S(2)}, u32[]{:S(2)}) %all-to-all-start) | async-done | bytes 12320 | tf_op jit(solution)/shard_map/all_to_all | solution.py:33
  106.7 0.9 copy.43
  107.5 0.8 slice.35
  108.4 5.1 %collective-permute-start.5 = (bf16[256,896]{1,0:T(8,128)(2,1)}, bf16[256,896]{1,0:T(8,128)(2,1)S(1)}, u32[]{:S(2)}, u32[]{:S(2)}) collective-permute-start(bf16[256,896]{1,0:T(8,128)(2,1)} %slice.35), channel_id=1, source_target_pairs={{16,0},{32,16},{48,32},{0,48},{17,1},{33,17},{49,33},{1,49},{18,2}... | collective-permute-start | bytes 1376264 | tf_op jit(solution)/shard_map/ppermute | solution.py:29
  113.5 0.8 collective-permute-done.6.before
  114.3 0.8 slice.36
  115.1 1.9 collective-permute-start.7
  117.1 1.5 copy-done.1
  118.6 1.5 copy-done.6
  120.1 1.5 copy-done.9
  121.6 1.8 copy-done.11
  123.4 7.6 %expert_up.2 = bf16[4,128,128]{2,1,0:T(8,128)(2,1)S(1)} custom-call(bf16[384,3584]{1,0:T(8,128)(2,1)S(1)} %copy-done.11, bf16[3584,256]{1,0:T(8,128)(2,1)S(1)} %copy-done.1, bf16[3584,256]{1,0:T(8,128)(2,1)S(1)} %copy-done.6, bf16[1792,256]{1,0:T(8,128)(2,1)} %collective-permute-done.1.far_top, bf16[1792,256]{1,0:T(8,128)(2,1)} %collective-permute-done.3.far_bottom, ...), custom_call_target="tpu_custom_call" | custom-call | flops 2818572288 | bytes 10092544 | tf_op jit(solution)/shard_map/expert_up/pallas_call | solution.py:107
  131.0 14.8 %all-gather = bf16[16,128,128]{2,1,0:T(8,128)(2,1)S(1)} all-gather(bf16[4,128,128]{2,1,0:T(8,128)(2,1)S(1)} %expert_up.2), channel_id=2, replica_groups=mesh['section'=8,'y'=4,'q'=4,'b'=4] {'b'}, dimensions={0}, use_global_device_ids=true | all-gather | bytes 655360 | tf_op jit(solution)/shard_map/all_gather | solution.py:218
  145.8 4.1 %expert_down.2 = bf16[384,896]{1,0:T(8,128)(2,1)S(1)} custom-call(bf16[4,4,128,128]{3,2,1,0:T(8,128)(2,1)S(1)} %bitcast.53, bf16[512,896]{1,0:T(8,128)(2,1)S(1)} %bitcast.49, bf16[512,896]{1,0:T(8,128)(2,1)S(1)} %collective-permute-done.4.after, bf16[256,896]{1,0:T(8,128)(2,1)S(1)} %collective-permute-done.5.far_top, ...), custom_call_target="tpu_custom_call" | custom-call | flops 1174405120 | bytes 4194304 | tf_op jit(solution)/shard_map/expert_down/pallas_call | solution.py:158
  150.0 48.6 %all_to_all.20.returned_ref = bf16[16,24,896]{2,1,0:T(8,128)(2,1)} all-to-all(bf16[16,24,896]{2,1,0:T(8,128)(2,1)S(1)} %bitcast.52), channel_id=1, replica_groups=mesh['section'=8,'y'=4,'q'=4,'b'=4] {'q','b'}, dimensions={0} | all-to-all | bytes 1376256 | tf_op jit(solution)/shard_map/all_to_all | solution.py:33
  198.6 2.0 leave.2
  200.6 1.5 collective-permute-start.8
  202.0 1.0 collective-permute-done.8.handed_ref
  203.1 0.7 copy-done.15
  203.7 1.8 enter.3
  206.0 0.9 copy.48
  206.9 71.5 %all-gather.7.cloned.1.call-done.tokens_ref = bf16[384,3584]{1,0:T(8,128)(2,1)} async-done(((bf16[24,3584]{1,0:T(8,128)(2,1)}), bf16[384,3584]{1,0:T(8,128)(2,1)}) %all-gather.7.cloned.1.call-update) | async-done | bytes 2752528 | tf_op jit(solution)/shard_map/all_gather | solution.py:216
  278.4 1.5 copy-done.2
  279.9 1.5 copy-done.7
  281.4 1.5 copy-done.10
  282.9 1.8 copy-done.12
  284.7 7.6 %expert_up.3 = bf16[4,128,128]{2,1,0:T(8,128)(2,1)S(1)} custom-call(bf16[384,3584]{1,0:T(8,128)(2,1)S(1)} %copy-done.12, bf16[3584,256]{1,0:T(8,128)(2,1)S(1)} %copy-done.2, bf16[3584,256]{1,0:T(8,128)(2,1)S(1)} %copy-done.7, bf16[1792,256]{1,0:T(8,128)(2,1)} %collective-permute-done.1.far_top, bf16[1792,256]{1,0:T(8,128)(2,1)} %collective-permute-done.3.far_bottom, ...), custom_call_target="tpu_custom_call" | custom-call | flops 2818572288 | bytes 10092544 | tf_op jit(solution)/shard_map/expert_up/pallas_call | solution.py:107
  292.3 13.6 %all-gather.1 = bf16[16,128,128]{2,1,0:T(8,128)(2,1)S(1)} all-gather(bf16[4,128,128]{2,1,0:T(8,128)(2,1)S(1)} %expert_up.3), channel_id=3, replica_groups=mesh['section'=8,'y'=4,'q'=4,'b'=4] {'b'}, dimensions={0}, use_global_device_ids=true | all-gather | bytes 655360 | tf_op jit(solution)/shard_map/all_gather | solution.py:218
  305.9 4.1 %expert_down.3 = bf16[384,896]{1,0:T(8,128)(2,1)S(1)} custom-call(bf16[4,4,128,128]{3,2,1,0:T(8,128)(2,1)S(1)} %bitcast.54, bf16[512,896]{1,0:T(8,128)(2,1)S(1)} %bitcast.50, bf16[512,896]{1,0:T(8,128)(2,1)S(1)} %collective-permute-done.4.after, bf16[256,896]{1,0:T(8,128)(2,1)S(1)} %collective-permute-done.5.far_top, ...), custom_call_target="tpu_custom_call" | custom-call | flops 1174405120 | bytes 4194304 | tf_op jit(solution)/shard_map/expert_down/pallas_call | solution.py:158
  310.0 35.2 %all_to_all.21.returned_ref = bf16[16,24,896]{2,1,0:T(8,128)(2,1)} all-to-all(bf16[16,24,896]{2,1,0:T(8,128)(2,1)S(1)} %bitcast.51), channel_id=1, replica_groups=mesh['section'=8,'y'=4,'q'=4,'b'=4] {'q','b'}, dimensions={0} | all-to-all | bytes 1376256 | tf_op jit(solution)/shard_map/all_to_all | solution.py:33
  345.2 2.0 leave.3
  (57 shorter events, 1.8 us)
Async XLA Ops:
  7.2 109.9 %all-gather.5.cloned.1.call-start = ((), (), s32[]{:S(2)}) async-start(), calls=%async_computation.4 | async-start | bytes 2924544 | tf_op jit(solution)/shard_map/all_gather | solution.py:216
  11.0 10.1 %copy-start.13 = (bf16[1,3584,128]{2,1,0:T(8,128)(2,1)S(1)}, bf16[1,3584,128]{2,1,0:T(8,128)(2,1)}, u32[]{:S(2)}) copy-start(bf16[1,3584,128]{2,1,0:T(8,128)(2,1)} %param.14) | copy-start | bytes 2752516
  11.0 10.0 %copy-start.14 = (bf16[1,3584,128]{2,1,0:T(8,128)(2,1)S(1)}, bf16[1,3584,128]{2,1,0:T(8,128)(2,1)}, u32[]{:S(2)}) copy-start(bf16[1,3584,128]{2,1,0:T(8,128)(2,1)} %param.13) | copy-start | bytes 2752516
  12.1 60.8 %all-to-all-start.1 = ((bf16[4,128,896]{2,1,0:T(8,128)(2,1)}), bf16[4,128,896]{2,1,0:T(8,128)(2,1)S(1)}, u32[]{:S(2)}, u32[]{:S(2)}) async-start(bf16[4,128,896]{2,1,0:T(8,128)(2,1)} %bitcast.46), calls=%async_computation.1 | async-start | bytes 1835008 | tf_op jit(solution)/shard_map/all_to_all | solution.py:33
  21.3 48.5 %copy-start = (bf16[3584,256]{1,0:T(8,128)(2,1)}, bf16[3584,256]{1,0:T(8,128)(2,1)S(1)}, u32[]{:S(2)}) copy-start(bf16[3584,256]{1,0:T(8,128)(2,1)S(1)} %pad_maximum_fusion.own) | copy-start | bytes 5505028
  21.3 58.8 %copy-start.16 = (s32[2,1,24,2]{2,3,1,0:T(2,128)S(1)}, s32[2,1,24,2]{2,3,1,0:T(2,128)}, u32[]{:S(2)}) copy-start(s32[2,1,24,2]{2,3,1,0:T(2,128)} %param.10) | copy-start | bytes 1156
  21.3 58.8 %copy-start.17 = (f32[2,1,24,2]{2,3,1,0:T(2,128)S(1)}, f32[2,1,24,2]{2,3,1,0:T(2,128)}, u32[]{:S(2)}) copy-start(f32[2,1,24,2]{2,3,1,0:T(2,128)} %param.11) | copy-start | bytes 1156
  21.3 40.8 %collective-permute-start = (bf16[3584,256]{1,0:T(8,128)(2,1)S(1)}, bf16[3584,256]{1,0:T(8,128)(2,1)S(1)}, u32[]{:S(2)}, u32[]{:S(2)}) collective-permute-start(bf16[3584,256]{1,0:T(8,128)(2,1)S(1)} %pad_maximum_fusion.own), channel_id=1, source_target_pairs={{16,0},{32,16},{48,32},{0,48},{17,1},{33,17},{49,33},{1,49},{18,2}... | collective-permute-start | bytes 5505032 | tf_op jit(solution)/shard_map/ppermute | solution.py:29
  23.4 45.3 %collective-permute-start.2 = (bf16[3584,256]{1,0:T(8,128)(2,1)S(1)}, bf16[3584,256]{1,0:T(8,128)(2,1)S(1)}, u32[]{:S(2)}, u32[]{:S(2)}) collective-permute-start(bf16[3584,256]{1,0:T(8,128)(2,1)S(1)} %pad_maximum_fusion.own), channel_id=1, source_target_pairs={{48,0},{0,16},{16,32},{32,48},{49,1},{1,17},{17,33},{33,49},{50,2}... | collective-permute-start | bytes 5505032 | tf_op jit(solution)/shard_map/ppermute | solution.py:29
  62.1 7.6 %copy-start.5 = (bf16[3584,256]{1,0:T(8,128)(2,1)}, bf16[3584,256]{1,0:T(8,128)(2,1)S(1)}, u32[]{:S(2)}) copy-start(bf16[3584,256]{1,0:T(8,128)(2,1)S(1)} %collective-permute-done.after) | copy-start | bytes 5505028
  63.2 53.9 %collective-permute-start.1 = (bf16[1792,256]{1,0:T(8,128)(2,1)}, bf16[1792,256]{1,0:T(8,128)(2,1)}, u32[]{:S(2)}, u32[]{:S(2)}) collective-permute-start(bf16[1792,256]{1,0:T(8,128)(2,1)} %slice.32), channel_id=1, source_target_pairs={{16,0},{32,16},{48,32},{0,48},{17,1},{33,17},{49,33},{1,49},{18,2}... | collective-permute-start | bytes 2752520 | tf_op jit(solution)/shard_map/ppermute | solution.py:29
  69.7 1.3 copy-start.8
  71.0 46.0 %collective-permute-start.3 = (bf16[1792,256]{1,0:T(8,128)(2,1)}, bf16[1792,256]{1,0:T(8,128)(2,1)}, u32[]{:S(2)}, u32[]{:S(2)}) collective-permute-start(bf16[1792,256]{1,0:T(8,128)(2,1)} %slice.33), channel_id=1, source_target_pairs={{48,0},{0,16},{16,32},{32,48},{49,1},{1,17},{17,33},{33,49},{50,2}... | collective-permute-start | bytes 2752520 | tf_op jit(solution)/shard_map/ppermute | solution.py:29
  73.0 34.6 %collective-permute-start.4 = (bf16[512,896]{1,0:T(8,128)(2,1)S(1)}, bf16[512,896]{1,0:T(8,128)(2,1)S(1)}, u32[]{:S(2)}, u32[]{:S(2)}) collective-permute-start(bf16[512,896]{1,0:T(8,128)(2,1)S(1)} %bitcast.47), channel_id=1, source_target_pairs={{16,0},{32,16},{48,32},{0,48},{17,1},{33,17},{49,33},{1,49},{18,2}... | collective-permute-start | bytes 2752520 | tf_op jit(solution)/shard_map/ppermute | solution.py:29
  78.1 36.2 %collective-permute-start.6 = (bf16[512,896]{1,0:T(8,128)(2,1)S(1)}, bf16[512,896]{1,0:T(8,128)(2,1)S(1)}, u32[]{:S(2)}, u32[]{:S(2)}) collective-permute-start(bf16[512,896]{1,0:T(8,128)(2,1)S(1)} %bitcast.48), channel_id=1, source_target_pairs={{48,0},{0,16},{16,32},{32,48},{49,1},{1,17},{17,33},{33,49},{50,2}... | collective-permute-start | bytes 2752520 | tf_op jit(solution)/shard_map/ppermute | solution.py:29
  80.9 24.8 %all-to-all-start = ((f32[16,1,192]{2,1,0:T(1,128)}), f32[16,1,192]{2,1,0:T(1,128)S(1)}, u32[]{:S(2)}, u32[]{:S(2)}) async-start(f32[16,1,192]{2,1,0:T(1,128)} %broadcast_in_dim.30), calls=%async_computation | async-start | bytes 32768 | tf_op jit(solution)/shard_map/all_to_all | solution.py:33
  94.5 184.0 %all-gather.7.cloned.1.call-start = ((), (), s32[]{:S(2)}) async-start(), calls=%async_computation.5 | async-start | bytes 2924544 | tf_op jit(solution)/shard_map/all_gather | solution.py:216
  108.4 37.5 %collective-permute-start.5 = (bf16[256,896]{1,0:T(8,128)(2,1)}, bf16[256,896]{1,0:T(8,128)(2,1)S(1)}, u32[]{:S(2)}, u32[]{:S(2)}) collective-permute-start(bf16[256,896]{1,0:T(8,128)(2,1)} %slice.35), channel_id=1, source_target_pairs={{16,0},{32,16},{48,32},{0,48},{17,1},{33,17},{49,33},{1,49},{18,2}... | collective-permute-start | bytes 1376264 | tf_op jit(solution)/shard_map/ppermute | solution.py:29
  115.1 30.7 %collective-permute-start.7 = (bf16[256,896]{1,0:T(8,128)(2,1)}, bf16[256,896]{1,0:T(8,128)(2,1)}, u32[]{:S(2)}, u32[]{:S(2)}) collective-permute-start(bf16[256,896]{1,0:T(8,128)(2,1)} %slice.36), channel_id=1, source_target_pairs={{48,0},{0,16},{16,32},{32,48},{49,1},{1,17},{17,33},{33,49},{50,2}... | collective-permute-start | bytes 1376264 | tf_op jit(solution)/shard_map/ppermute | solution.py:29
  117.1 1.5 copy-start.1
  118.6 1.5 copy-start.6
  120.1 1.5 copy-start.9
  121.6 1.8 copy-start.11
  123.4 22.5 %copy-start.3 = (f32[4,16,24]{0,2,1:T(8,128)S(1)}, f32[4,16,24]{0,2,1:T(8,128)}, u32[]{:S(2)}) copy-start(f32[4,16,24]{0,2,1:T(8,128)} %copy.43) | copy-start | bytes 18436
  200.6 2.5 collective-permute-start.8
  203.1 0.7 copy-start.15
  278.4 1.5 copy-start.2
  279.9 1.5 copy-start.7
  281.4 1.5 copy-start.10
  282.9 1.8 copy-start.12
  284.7 21.2 %copy-start.4 = (f32[4,16,24]{0,2,1:T(8,128)S(1)}, f32[4,16,24]{0,2,1:T(8,128)}, u32[]{:S(2)}) copy-start(f32[4,16,24]{0,2,1:T(8,128)} %copy.48) | copy-start | bytes 18436
Sparse Core Ops, SparseCore 0:
  10.7 83.4 all-gather.4
  205.7 72.6 all-gather.6

commit v4 on v2

v4 whole, which is shorter than its diff:
```python
import functools

import jax
import jax.numpy as jnp
from jax import lax
from jax.experimental import pallas as pl
from jax.experimental.pallas import tpu as pltpu
from jax.sharding import Mesh, PartitionSpec as P

TOPK = 2
HS = 8
QUARTERS = 4


HIGH = lax.Precision.HIGHEST
RING = ("q", "b")
STORE = ("y",) + RING
MIB = 1 << 20
LANES = 128
SUBLANES = 8


def shifted(shard, axis, by):
    peers = lax.axis_size(axis)
    pairs = [(i, i + by) for i in range(peers) if 0 <= i + by < peers]
    return lax.ppermute(shard, axis, pairs)


def fetched(shard, axis, ahead):
    peers = lax.axis_size(axis)
    return lax.ppermute(shard, axis, [((i + ahead) % peers, i) for i in range(peers)])


def swap(blocks, axis):
    return lax.all_to_all(blocks, axis, split_axis=0, concat_axis=0, tiled=True)


def send_rows(tick, acts, gain_ref, routes_ref, gates_ref, sent_ref, table):
    rows, width = acts.shape
    values = acts.astype(jnp.float32)
    scale = lax.rsqrt(jnp.mean(values * values, axis=-1, keepdims=True) + 1e-06)
    sent_ref[:, :width] = (values * scale * gain_ref[...]).astype(jnp.bfloat16)
    gates = gates_ref[tick]
    high = gates.astype(jnp.bfloat16).astype(jnp.float32)
    middle = (gates - high).astype(jnp.bfloat16).astype(jnp.float32)
    table[...] = jnp.zeros_like(table)
    table[0:2, 0:rows] = routes_ref[tick].astype(jnp.float32)
    table[2:4, 0:rows] = high
    table[4:6, 0:rows] = middle
    table[6:8, 0:rows] = gates - high - middle
    sent_ref[:, width:] = table[...].T[0:rows].astype(jnp.bfloat16)


def entry_kernel(
    first_ref, fed_ref, handed_ref, gain_ref, routes_ref, gates_ref, entry_ref, sent_ref, table
):
    acts = jnp.where(first_ref[0] == 1, fed_ref[...], handed_ref[...])
    entry_ref[...] = acts
    send_rows(1, acts, gain_ref, routes_ref, gates_ref, sent_ref, table)


def start_kernel(acts_ref, gain_ref, routes_ref, gates_ref, sent_ref, table):
    send_rows(0, acts_ref[...], gain_ref, routes_ref, gates_ref, sent_ref, table)


def start(acts, gain, routes, gates):
    vmem = pl.BlockSpec(memory_space=pltpu.VMEM)
    rows, width = acts.shape
    return pl.pallas_call(
        start_kernel,
        out_shape=jax.ShapeDtypeStruct((rows, width + LANES), jnp.bfloat16),
        in_specs=[vmem] * 4,
        out_specs=vmem,
        scratch_shapes=[pltpu.VMEM((LANES, LANES), jnp.float32)],
        cost_estimate=pl.CostEstimate(
            flops=6 * acts.size, bytes_accessed=8 * acts.size, transcendentals=0
        ),
        name="start",
    )(acts, gain, routes, gates)


def part_kernel(down_ref, parted_ref, sems):
    part = parted_ref.shape[2]
    copies = [
        pltpu.make_async_copy(down_ref.at[:, pl.ds(i * part, part)], parted_ref.at[i], sems.at[i])
        for i in range(QUARTERS)
    ]
    for copy in copies:
        copy.start()
    for copy in copies:
        copy.wait()


def in_parts(down_w):
    rows, width = down_w.shape
    return pl.pallas_call(
        part_kernel,
        out_shape=jax.ShapeDtypeStruct((QUARTERS, rows, width // QUARTERS), jnp.bfloat16),
        in_specs=[pl.BlockSpec(memory_space=pltpu.HBM)],
        out_specs=pl.BlockSpec(memory_space=pltpu.VMEM),
        scratch_shapes=[pltpu.SemaphoreType.DMA((QUARTERS,))],
        cost_estimate=pl.CostEstimate(flops=0, bytes_accessed=4 * down_w.size, transcendentals=0),
        name="in_parts",
    )(down_w)


def enter(is_first, fed, handed, gain, routes, gates):
    vmem = pl.BlockSpec(memory_space=pltpu.VMEM)
    rows, width = fed.shape
    return pl.pallas_call(
        entry_kernel,
        out_shape=(
            jax.ShapeDtypeStruct((rows, width), jnp.bfloat16),
            jax.ShapeDtypeStruct((rows, width + LANES), jnp.bfloat16),
        ),
        in_specs=[pl.BlockSpec(memory_space=pltpu.SMEM)] + [vmem] * 5,
        out_specs=(vmem, vmem),
        scratch_shapes=[pltpu.VMEM((LANES, LANES), jnp.float32)],
        cost_estimate=pl.CostEstimate(flops=6 * fed.size, bytes_accessed=8 * fed.size, transcendentals=0),
        name="enter",
    )(is_first, fed, handed, gain, routes, gates)


def slot_tables(facts, wanted_ref, block_rows, capacity):
    rows = facts.shape[0]
    shape = (SUBLANES, LANES)
    which = lax.broadcasted_iota(jnp.int32, shape, 0)
    column = lax.broadcasted_iota(jnp.int32, shape, 1)
    same = (column < 8) & (
        ((which < 2) & (column == which))
        | ((which >= 2) & (which < 4) & (column >= 2) & (column % 2 == which % 2))
    )
    told = lax.dot_general(
        jnp.where(same, 1.0, 0.0).astype(jnp.bfloat16),
        facts,
        (((1,), (1,)), ((), ())),
        preferred_element_type=jnp.float32,
    )
    ahead = lax.broadcasted_iota(jnp.int32, (SUBLANES, rows), 0)
    wanted = jnp.full((SUBLANES, rows), -9, jnp.int32)
    for i in range(QUARTERS):
        wanted = jnp.where(ahead == i, wanted_ref[i], wanted)
    wanted = wanted.astype(jnp.float32)
    first = told[0:1, :] == wanted
    second = told[1:2, :] == wanted
    gate = jnp.where(first, told[2:3, :], 0.0) + jnp.where(second, told[3:4, :], 0.0)
    hit = first | second
    source = lax.broadcasted_iota(jnp.int32, (rows, rows), 0)
    target = lax.broadcasted_iota(jnp.int32, (rows, rows), 1)
    blocks = rows // block_rows
    start = jnp.zeros((1, rows), jnp.int32)
    lane = lax.broadcasted_iota(jnp.int32, (1, rows), 1)
    for i in range(1, blocks):
        start = jnp.where(lane >= i * block_rows, i * block_rows, start)
    earlier = (source < target) & (source >= start)
    position = jnp.dot(
        jnp.where(hit, 1.0, 0.0).astype(jnp.bfloat16),
        jnp.where(earlier, 1.0, 0.0).astype(jnp.bfloat16),
        preferred_element_type=jnp.float32,
    ).astype(jnp.int32)
    base = jnp.zeros((1, rows), jnp.int32)
    for i in range(1, blocks):
        base = jnp.where(lane >= i * block_rows, i * capacity, base)
    return (jnp.where(hit, base + position, -1), gate)


def up_kernel(
    capacity, block_rows, wanted_ref, tokens_ref, own_g, own_u, after_g, after_u, far_g, far_u,
    before_g, before_u, packed_ref, place_ref, gate_ref, tokens, weights, sems, token_sem,
):
    token_copy = pltpu.make_async_copy(tokens_ref, tokens, token_sem)
    token_copy.start()
    pieces = (own_g, own_u, after_g, after_u, far_g, far_u, before_g, before_u)
    copies = [pltpu.make_async_copy(pieces[i], weights.at[i], sems.at[i]) for i in range(2 * QUARTERS)]
    for copy in copies[:4]:
        copy.start()
    token_copy.wait()
    rows = tokens.shape[0]
    width = tokens.shape[1] - LANES
    slots = packed_ref.shape[1]
    place, gate = slot_tables(tokens[:, width:], wanted_ref, block_rows, capacity)
    place_ref[...] = place
    gate_ref[...] = gate
    slot = lax.broadcasted_iota(jnp.int32, (slots, rows), 0)
    pack = jnp.concatenate(
        [
            jnp.where(slot == place[ahead : ahead + 1, :], 1.0, 0.0).astype(jnp.bfloat16)
            for ahead in range(QUARTERS)
        ],
        axis=0,
    )
    sent = jnp.dot(pack, tokens[:, :width], preferred_element_type=jnp.float32).astype(jnp.bfloat16)
    for ahead in range(QUARTERS):
        copies[2 * ahead].wait()
        copies[2 * ahead + 1].wait()
        if ahead < 2:
            copies[2 * ahead + 4].start()
            copies[2 * ahead + 5].start()
        mine = sent[ahead * slots : (ahead + 1) * slots]
        both = jnp.concatenate([weights[2 * ahead], weights[2 * ahead + 1]], axis=1)
        inner = jnp.dot(
            mine[:, : width // 2], both[: width // 2], preferred_element_type=jnp.float32
        )
        inner = inner + jnp.dot(
            mine[:, width // 2 :], both[width // 2 :], preferred_element_type=jnp.float32
        )
        units = inner.shape[1] // 2
        gates = inner[:, :units]
        hidden = gates / (1.0 + jnp.exp(-gates)) * inner[:, units:]
        packed_ref[ahead] = hidden.astype(jnp.bfloat16)


def expert_up(tokens, wanted, in_w, slots, block_rows):
    rows = tokens.shape[0]
    width, units = in_w[0].shape
    capacity = slots * block_rows // rows
    in_hbm = pl.BlockSpec(memory_space=pltpu.HBM)
    vmem = pl.BlockSpec(memory_space=pltpu.VMEM)
    return pl.pallas_call(
        functools.partial(up_kernel, capacity, block_rows),
        out_shape=(
            jax.ShapeDtypeStruct((QUARTERS, slots, units), jnp.bfloat16),
            jax.ShapeDtypeStruct((SUBLANES, rows), jnp.int32),
            jax.ShapeDtypeStruct((SUBLANES, rows), jnp.float32),
        ),
        in_specs=[pl.BlockSpec(memory_space=pltpu.SMEM)] + [in_hbm] * 9,
        out_specs=(vmem, vmem, vmem),
        scratch_shapes=[
            pltpu.VMEM(tokens.shape, jnp.bfloat16),
            pltpu.VMEM((2 * QUARTERS, width, units), jnp.bfloat16),
            pltpu.SemaphoreType.DMA((2 * QUARTERS,)),
            pltpu.SemaphoreType.DMA,
        ],
        compiler_params=pltpu.CompilerParams(vmem_limit_bytes=60 * MIB),
        cost_estimate=pl.CostEstimate(
            flops=2 * QUARTERS * slots * width * (2 * units + rows),
            bytes_accessed=2 * width * (rows + 2 * QUARTERS * units),
            transcendentals=QUARTERS * slots * units,
        ),
        name="expert_up",
    )(wanted, tokens, *in_w)


def down_kernel(
    hidden_ref, own, after, far, before, place_ref, gate_ref, out_ref, weights, parts, sems
):
    copies = [
        pltpu.make_async_copy(piece, weights.at[ahead], sems.at[ahead])
        for ahead, piece in enumerate((own, after, far, before))
    ]
    for copy in copies:
        copy.start()
    rows = out_ref.shape[0]
    slots = hidden_ref.shape[2]
    slot = lax.broadcasted_iota(jnp.int32, (slots, rows), 0)
    pack = []
    for ahead in range(QUARTERS):
        copies[ahead].wait()
        units = jnp.concatenate([hidden_ref[b, ahead] for b in range(QUARTERS)], axis=1)
        out = jnp.dot(units, weights[ahead], preferred_element_type=jnp.float32)
        here = slot == place_ref[ahead : ahead + 1, :]
        gate = jnp.sum(jnp.where(here, gate_ref[ahead : ahead + 1, :], 0.0), axis=1, keepdims=True)
        out = out * gate
        high = out.astype(jnp.bfloat16)
        parts[0, pl.ds(ahead * slots, slots)] = high
        parts[1, pl.ds(ahead * slots, slots)] = (out - high.astype(jnp.float32)).astype(jnp.bfloat16)
        pack.append(jnp.where(here, 1.0, 0.0))
    unpack = jnp.concatenate(pack, axis=0).T.astype(jnp.bfloat16)
    mixed = jnp.dot(unpack, parts[0], preferred_element_type=jnp.float32)
    mixed = mixed + jnp.dot(unpack, parts[1], preferred_element_type=jnp.float32)
    out_ref[...] = mixed.astype(jnp.bfloat16)


def expert_down(hidden, out_w, place, gate):
    rows = place.shape[1]
    units, part = out_w[0].shape
    slots = hidden.shape[2]
    in_hbm = pl.BlockSpec(memory_space=pltpu.HBM)
    vmem = pl.BlockSpec(memory_space=pltpu.VMEM)
    return pl.pallas_call(
        down_kernel,
        out_shape=jax.ShapeDtypeStruct((rows, part), jnp.bfloat16),
        in_specs=[vmem] + [in_hbm] * 4 + [vmem] * 2,
        out_specs=vmem,
        scratch_shapes=[
            pltpu.VMEM((QUARTERS, units, part), jnp.bfloat16),
            pltpu.VMEM((2, QUARTERS * slots, part), jnp.bfloat16),
            pltpu.SemaphoreType.DMA((QUARTERS,)),
        ],
        compiler_params=pltpu.CompilerParams(vmem_limit_bytes=60 * MIB),
        cost_estimate=pl.CostEstimate(
            flops=2 * QUARTERS * slots * part * (units + 2 * rows),
            bytes_accessed=2 * QUARTERS * units * (part + slots),
            transcendentals=0,
        ),
        name="expert_down",
    )(hidden, *out_w, place, gate)


def leave_kernel(entry_ref, returned_ref, out_ref):
    part = returned_ref.shape[2]
    for b in range(QUARTERS):
        columns = pl.ds(b * part, part)
        total = entry_ref[:, columns].astype(jnp.float32)
        for q in range(returned_ref.shape[0] // QUARTERS):
            total = total + returned_ref[q * QUARTERS + b].astype(jnp.float32)
        out_ref[:, columns] = total.astype(jnp.bfloat16)


def leave(entry, returned):
    vmem = pl.BlockSpec(memory_space=pltpu.VMEM)
    return pl.pallas_call(
        leave_kernel,
        out_shape=jax.ShapeDtypeStruct(entry.shape, jnp.bfloat16),
        in_specs=[vmem] * 2,
        out_specs=vmem,
        cost_estimate=pl.CostEstimate(
            flops=returned.size, bytes_accessed=2 * returned.size + 4 * entry.size, transcendentals=0
        ),
        name="leave",
    )(entry, returned)


def layer(entry, sent, wanted, in_w, out_w, slots):
    rows, width = entry.shape
    tokens = lax.all_gather(sent, RING, tiled=True)
    hidden, place, gate = expert_up(tokens, wanted, in_w, slots, rows)
    hidden = lax.all_gather(hidden, "b", axis=0)
    mixed = expert_down(hidden, out_w, place, gate)
    returned = swap(mixed.reshape(-1, rows, width // QUARTERS), RING)
    return leave(entry, returned)


def on_device(hidden_in, incoming, routes, gates, norm_gain, w_gate, w_up, w_down):
    section_place = lax.axis_index("section")
    rows, width = incoming.shape
    n_store = lax.axis_size(STORE)
    experts = n_store // HS
    capacity = HS * ((rows * TOPK + experts * HS - 1) // (experts * HS))
    part = width // QUARTERS
    ring = lax.axis_size(RING)
    slots = ring * capacity
    routes, gates = [jnp.swapaxes(a[:, 0], 1, 2) for a in (routes, gates)]
    sent = start(hidden_in[0], norm_gain, routes, gates)
    parted = in_parts(w_down[0])

    gate_w, up_w = w_gate[0], w_up[0]
    after_gate = fetched(gate_w, "y", 1)
    before_up = fetched(up_w, "y", 3)
    after_up = fetched(up_w, "y", 1)
    before_gate = fetched(gate_w, "y", 3)
    far_up = fetched(after_up, "y", 1)
    far_gate = fetched(before_gate, "y", 3)
    in_w = (gate_w, up_w, after_gate, after_up, far_gate, far_up, before_gate, before_up)
    out_w = swap(parted, "b").reshape(-1, part)
    out_w, _, _ = lax.optimization_barrier((out_w, after_gate, before_up))
    out_w = (out_w,) + tuple(fetched(out_w, "y", ahead) for ahead in (1, 2, 3))
    ring_place = lax.axis_index(RING)
    y_place = (lax.axis_index("y") + jnp.arange(QUARTERS, dtype=jnp.int32)) % QUARTERS
    wanted = y_place * (ring // HS) + ring_place // HS
    first = layer(hidden_in[0], sent, wanted, in_w, out_w, slots)
    handed = shifted(first, "section", 1)
    is_first = (section_place == 0).astype(jnp.int32).reshape(1)
    entry, sent = enter(is_first, incoming, handed, norm_gain, routes, gates)
    second = layer(entry, sent, wanted, in_w, out_w, slots)
    return (first[None], second[None])


def solution(mesh):
    sections, stores = mesh.devices.shape
    fine = Mesh(
        mesh.devices.reshape(sections, 4, stores // (4 * QUARTERS), QUARTERS),
        ("section",) + STORE,
    )
    placed = (
        P("section", STORE, None),
        P(STORE, None),
        P(None, "section", STORE, None),
        P(None, "section", STORE, None),
        P("section", None),
        P("section", None, STORE),
        P("section", None, STORE),
        P("section", STORE, None),
    )
    return jax.shard_map(
        on_device,
        mesh=fine,
        in_specs=placed,
        out_specs=(P("section", STORE, None), P("section", STORE, None)),
        check_vma=False,
    )
```

time: 367 us -> 333 us (0.907)
  matrix products: 42.2 us -> 0 us
  Pallas kernels: 0 us -> 38.8 us
  local copies, waits for them, and re-layouts: 19 us -> 2.84 us
  blocking collectives: 118 us -> 106 us
  other arithmetic: 10.9 us -> 0.61 us
  waiting for transfers between devices: 123 us -> 128 us
    ppermute x6 -> x9, waiting for transfers between devices: 10.1 us -> 54.4 us  [fetched(): lax.ppermute(shard, axis, [((i + ahead) % peers, i) for i in range(peers)])]
    dot_general x34 -> x0, matrix products: 42.2 us -> none  [the longest x8 18.1 us: layer(): inner = jnp.dot(tokens, in_w[ahead], preferred_element_type=jnp.float32)]
    all_gather x3 -> x2, blocking collectives: 69.6 us -> 30.2 us  [layer(): hidden = lax.all_gather(hidden, 'b', axis=0)]
    pallas_call x0 -> x9, Pallas kernels: none -> 38.8 us  [the longest x2 18.5 us: expert_up(): pl.pallas_call(functools.partial(up_kernel, capacity, block_rows), out_sh...]
    all_to_all x1 -> x2, blocking collectives: 48 us -> 76 us  [swap(): return lax.all_to_all(blocks, axis, split_axis=0, concat_axis=0, tiled=True)]
    all_to_all x2 -> x1, waiting for transfers between devices: 22.1 us -> 0.01 us  [swap(): return lax.all_to_all(blocks, axis, split_axis=0, concat_axis=0, tiled=True)]
    all_gather x2, waiting for transfers between devices: 89.9 us -> 72.7 us  [layer(): tokens = lax.all_gather(sent, RING, tiled=True)]
    ppermute x6 -> x9, starting transfers between devices: 19.2 us -> 30.8 us  [fetched(): lax.ppermute(shard, axis, [((i + ahead) % peers, i) for i in range(peers)])]
  transfers between devices with their start and end apart: 11 -> 13, of which waited for: 6 -> 6; matrix products, arithmetic and copies ran while one was open for 10% -> 0% of each run, Pallas kernels for 0% -> 3%
where the time goes in v4:
time: 333 us; the launch traced here: 332 us
  waiting for transfers between devices  128 us (38%)
  blocking collectives  106 us (32%)
  starting transfers between devices  41.1 us (12%)
  Pallas kernels  38.8 us (12%)
  between operations  14.2 us (4%)
    all_to_all x2, blocking collectives, swap(): return lax.all_to_all(blocks, axis, split_axis=0, concat_axis=0, tiled=True)  76 us
    all_gather x2, waiting for transfers between devices, layer(): tokens = lax.all_gather(sent, RING, tiled=True)  72.7 us
    ppermute x9, waiting for transfers between devices, fetched(): lax.ppermute(shard, axis, [((i + ahead) % peers, i) for i in range(peers)])  54.4 us
    ppermute x9, starting transfers between devices, fetched(): lax.ppermute(shard, axis, [((i + ahead) % peers, i) for i in range(peers)])  30.8 us
    all_gather x2, blocking collectives, layer(): hidden = lax.all_gather(hidden, 'b', axis=0)  30.2 us
    pallas_call x2, Pallas kernels, expert_up(): pl.pallas_call(functools.partial(up_kernel, capacity, block_rows), out_sh...  18.5 us
    pallas_call x2, Pallas kernels, expert_down(): pl.pallas_call(down_kernel, out_shape=jax.ShapeDtypeStruct((rows, part),...  10.5 us
    all_to_all x1, starting transfers between devices, swap(): return lax.all_to_all(blocks, axis, split_axis=0, concat_axis=0, tiled=True)  8.97 us
  transfers between devices with their start and end apart: 13, of which 6 were waited for; matrix products, arithmetic and copies ran while one was open for 0% of the time, Pallas kernels for 3%

profile of v4, /device:TPU:32, one launch (start us, length us, event | category | flops | bytes accessed | tf_op | source)
XLA Modules:
  0.0 332.2 jit_solution(5141467439858234223)
XLA Ops:
  7.2 0.0 copy-start.1
  7.2 0.0 copy-start.2
  7.2 0.0 all-gather.5.cloned.1.call-start
  7.2 1.9 start.1
  9.1 0.0 all-gather.5.cloned.1.call-update
  9.1 2.3 in_parts.1
  11.4 9.0 %all-to-all-start = ((bf16[4,128,896]{2,1,0:T(8,128)(2,1)}), bf16[4,128,896]{2,1,0:T(8,128)(2,1)S(1)}, u32[]{:S(2)}, u32[]{:S(2)}) async-start(bf16[4,128,896]{2,1,0:T(8,128)(2,1)} %in_parts.1), calls=%async_computation | async-start | bytes 1835008 | tf_op jit(solution)/shard_map/all_to_all | solution.py:35
  20.4 0.0 all-gather.7.cloned.1.call-start
  20.4 1.9 collective-permute-start.2
  22.3 5.1 %collective-permute-start.1 = (bf16[3584,128]{1,0:T(8,128)(2,1)S(1)}, bf16[3584,128]{1,0:T(8,128)(2,1)}, u32[]{:S(2)}, u32[]{:S(2)}) collective-permute-start(bf16[3584,128]{1,0:T(8,128)(2,1)S(1)} %bitcast.29), channel_id=1, source_target_pairs={{16,0},{32,16},{48,32},{0,48},{17,1},{33,17},{49,33},{1,49},{18,2}... | collective-permute-start | bytes 2752520 | tf_op jit(solution)/shard_map/ppermute | solution.py:31
  27.4 1.9 collective-permute-start
  29.4 3.9 %collective-permute-start.5 = (bf16[3584,128]{1,0:T(8,128)(2,1)S(1)}, bf16[3584,128]{1,0:T(8,128)(2,1)}, u32[]{:S(2)}, u32[]{:S(2)}) collective-permute-start(bf16[3584,128]{1,0:T(8,128)(2,1)S(1)} %bitcast.30), channel_id=1, source_target_pairs={{48,0},{0,16},{16,32},{32,48},{49,1},{1,17},{17,33},{33,49},{50,2}... | collective-permute-start | bytes 2752520 | tf_op jit(solution)/shard_map/ppermute | solution.py:31
  33.3 13.6 %collective-permute-done.2.before_g = bf16[3584,128]{1,0:T(8,128)(2,1)} collective-permute-done((bf16[3584,128]{1,0:T(8,128)(2,1)S(1)}, bf16[3584,128]{1,0:T(8,128)(2,1)}, u32[]{:S(2)}, u32[]{:S(2)}) %collective-permute-start.2) | collective-permute-done | bytes 917536 | tf_op jit(solution)/shard_map/ppermute | solution.py:31
  46.9 1.9 collective-permute-start.3
  48.8 0.0 collective-permute-done.1.after_u
  48.8 5.1 %collective-permute-start.4 = (bf16[3584,128]{1,0:T(8,128)(2,1)}, bf16[3584,128]{1,0:T(8,128)(2,1)}, u32[]{:S(2)}, u32[]{:S(2)}) collective-permute-start(bf16[3584,128]{1,0:T(8,128)(2,1)} %collective-permute-done.1.after_u), channel_id=1, source_target_pairs={{16,0},{32,16},{48,32},{0,48},{17,1},{33,17},{49,33},{1,49},{18,2}... | collective-permute-start | bytes 2752520 | tf_op jit(solution)/shard_map/ppermute | solution.py:31
  53.9 14.0 %collective-permute-done.after_g = bf16[3584,128]{1,0:T(8,128)(2,1)S(1)} collective-permute-done((bf16[3584,128]{1,0:T(8,128)(2,1)S(1)}, bf16[3584,128]{1,0:T(8,128)(2,1)S(1)}, u32[]{:S(2)}, u32[]{:S(2)}) %collective-permute-start) | collective-permute-done | bytes 917536 | tf_op jit(solution)/shard_map/ppermute | solution.py:31
  67.9 1.0 copy-done.3
  68.9 0.0 collective-permute-done.5.before_u
  68.9 0.0 all-to-all-done
  68.9 1.9 collective-permute-start.8
  70.8 7.1 %collective-permute-start.7 = (bf16[512,896]{1,0:T(8,128)(2,1)S(1)}, bf16[512,896]{1,0:T(8,128)(2,1)S(1)}, u32[]{:S(2)}, u32[]{:S(2)}) collective-permute-start(bf16[512,896]{1,0:T(8,128)(2,1)S(1)} %bitcast.19), channel_id=1, source_target_pairs={{32,0},{48,16},{0,32},{16,48},{33,1},{49,17},{1,33},{17,49},{34,2}... | collective-permute-start | bytes 2752520 | tf_op jit(solution)/shard_map/ppermute | solution.py:31
  77.8 1.9 collective-permute-start.6
  79.8 0.6 fusion.1.wanted_ref
  80.4 5.8 %collective-permute-done.3.far_g = bf16[3584,128]{1,0:T(8,128)(2,1)} collective-permute-done((bf16[3584,128]{1,0:T(8,128)(2,1)}, bf16[3584,128]{1,0:T(8,128)(2,1)}, u32[]{:S(2)}, u32[]{:S(2)}) %collective-permute-start.3) | collective-permute-done | bytes 917536 | tf_op jit(solution)/shard_map/ppermute | solution.py:31
  86.2 21.1 %collective-permute-done.4.far_u = bf16[3584,128]{1,0:T(8,128)(2,1)} collective-permute-done((bf16[3584,128]{1,0:T(8,128)(2,1)}, bf16[3584,128]{1,0:T(8,128)(2,1)}, u32[]{:S(2)}, u32[]{:S(2)}) %collective-permute-start.4) | collective-permute-done | bytes 917536 | tf_op jit(solution)/shard_map/ppermute | solution.py:31
  107.3 9.2 %expert_up.2 = (bf16[4,128,128]{2,1,0:T(8,128)(2,1)}, s32[8,384]{1,0:T(8,128)}, f32[8,384]{1,0:T(8,128)}) custom-call(s32[4]{0:T(128)} %fusion.1.wanted_ref, bf16[384,3712]{1,0:T(8,128)(2,1)} %all-gather.5.cloned.1.call-done.tokens_ref, bf16[3584,128]{1,0:T(8,128)(2,1)} %bitcast.23, bf16[3584,128]{1,0:T(8,128)(2,1)} %bitcast.27, ...), custom_call_target="tpu_custom_call" | custom-call | flops 2348810240 | bytes 10092544 | tf_op jit(solution)/shard_map/expert_up/pallas_call | solution.py:219
  116.6 15.6 %all-gather = bf16[16,128,128]{2,1,0:T(8,128)(2,1)} all-gather(bf16[4,128,128]{2,1,0:T(8,128)(2,1)} %get-tuple-element.11), channel_id=2, replica_groups=mesh['section'=8,'y'=4,'q'=4,'b'=4] {'b'}, dimensions={0}, use_global_device_ids=true | all-gather | bytes 655360 | tf_op jit(solution)/shard_map/all_gather | solution.py:328
  132.2 0.0 collective-permute-done.8.before
  132.2 0.0 collective-permute-done.7.far
  132.2 0.0 copy-start.5
  132.2 0.0 collective-permute-done.6.after
  132.2 0.9 copy-done.4
  133.1 0.3 copy-done.5
  133.4 5.2 %expert_down.2 = bf16[384,896]{1,0:T(8,128)(2,1)} custom-call(bf16[4,4,128,128]{3,2,1,0:T(8,128)(2,1)} %bitcast.33, bf16[512,896]{1,0:T(8,128)(2,1)} %bitcast.21, bf16[512,896]{1,0:T(8,128)(2,1)} %collective-permute-done.6.after, bf16[512,896]{1,0:T(8,128)(2,1)} %copy-done.5, bf16[512,896]{1,0:T(8,128)(2,1)} %copy-done.4, ...), custom_call_target="tpu_custom_call" | custom-call | flops 1174405120 | bytes 4194304 | tf_op jit(solution)/shard_map/expert_down/pallas_call | solution.py:280
  138.7 40.3 %all_to_all.15.returned_ref = bf16[16,24,896]{2,1,0:T(8,128)(2,1)} all-to-all(bf16[16,24,896]{2,1,0:T(8,128)(2,1)} %bitcast.32), channel_id=1, replica_groups=mesh['section'=8,'y'=4,'q'=4,'b'=4] {'q','b'}, dimensions={0} | all-to-all | bytes 1376256 | tf_op jit(solution)/shard_map/all_to_all | solution.py:35
  178.9 2.0 leave.2
  180.9 1.3 collective-permute-start.9
  182.2 1.2 collective-permute-done.9.handed_ref
  183.4 0.7 copy-done.6
  184.1 1.8 enter.1
  185.9 0.0 all-gather.7.cloned.1.call-update
  185.9 72.7 %all-gather.7.cloned.1.call-done.tokens_ref = bf16[384,3712]{1,0:T(8,128)(2,1)} async-done(((bf16[24,3712]{1,0:T(8,128)(2,1)}), bf16[384,3712]{1,0:T(8,128)(2,1)}) %all-gather.7.cloned.1.call-update) | async-done | bytes 2850832 | tf_op jit(solution)/shard_map/all_gather | solution.py:326
  258.6 9.2 %expert_up.3 = (bf16[4,128,128]{2,1,0:T(8,128)(2,1)}, s32[8,384]{1,0:T(8,128)}, f32[8,384]{1,0:T(8,128)}) custom-call(s32[4]{0:T(128)} %fusion.1.wanted_ref, bf16[384,3712]{1,0:T(8,128)(2,1)} %all-gather.7.cloned.1.call-done.tokens_ref, bf16[3584,128]{1,0:T(8,128)(2,1)} %bitcast.24, bf16[3584,128]{1,0:T(8,128)(2,1)} %bitcast.28, ...), custom_call_target="tpu_custom_call" | custom-call | flops 2348810240 | bytes 10092544 | tf_op jit(solution)/shard_map/expert_up/pallas_call | solution.py:219
  267.8 14.6 %all-gather.1 = bf16[16,128,128]{2,1,0:T(8,128)(2,1)} all-gather(bf16[4,128,128]{2,1,0:T(8,128)(2,1)} %get-tuple-element.17), channel_id=3, replica_groups=mesh['section'=8,'y'=4,'q'=4,'b'=4] {'b'}, dimensions={0}, use_global_device_ids=true | all-gather | bytes 655360 | tf_op jit(solution)/shard_map/all_gather | solution.py:328
  282.4 5.2 %expert_down.3 = bf16[384,896]{1,0:T(8,128)(2,1)} custom-call(bf16[4,4,128,128]{3,2,1,0:T(8,128)(2,1)} %bitcast.34, bf16[512,896]{1,0:T(8,128)(2,1)} %bitcast.22, bf16[512,896]{1,0:T(8,128)(2,1)} %collective-permute-done.6.after, bf16[512,896]{1,0:T(8,128)(2,1)} %copy-done.5, bf16[512,896]{1,0:T(8,128)(2,1)} %copy-done.4, ...), custom_call_target="tpu_custom_call" | custom-call | flops 1174405120 | bytes 4194304 | tf_op jit(solution)/shard_map/expert_down/pallas_call | solution.py:280
  287.7 35.8 %all_to_all.16.returned_ref = bf16[16,24,896]{2,1,0:T(8,128)(2,1)} all-to-all(bf16[16,24,896]{2,1,0:T(8,128)(2,1)} %bitcast.31), channel_id=1, replica_groups=mesh['section'=8,'y'=4,'q'=4,'b'=4] {'q','b'}, dimensions={0} | all-to-all | bytes 1376256 | tf_op jit(solution)/shard_map/all_to_all | solution.py:35
  323.4 2.0 leave.3
  (8 shorter events, 0.0 us)
Async XLA Ops:
  7.2 13.2 %copy-start.1 = (bf16[1,3584,128]{2,1,0:T(8,128)(2,1)S(1)}, bf16[1,3584,128]{2,1,0:T(8,128)(2,1)}, u32[]{:S(2)}) copy-start(bf16[1,3584,128]{2,1,0:T(8,128)(2,1)} %param.13) | copy-start | bytes 2752516
  7.2 15.1 %copy-start.2 = (bf16[1,3584,128]{2,1,0:T(8,128)(2,1)S(1)}, bf16[1,3584,128]{2,1,0:T(8,128)(2,1)}, u32[]{:S(2)}) copy-start(bf16[1,3584,128]{2,1,0:T(8,128)(2,1)} %param.14) | copy-start | bytes 2752516
  7.2 100.1 %all-gather.5.cloned.1.call-start = ((), (), s32[]{:S(2)}) async-start(), calls=%async_computation.3 | async-start | bytes 3028992 | tf_op jit(solution)/shard_map/all_gather | solution.py:326
  11.4 57.5 %all-to-all-start = ((bf16[4,128,896]{2,1,0:T(8,128)(2,1)}), bf16[4,128,896]{2,1,0:T(8,128)(2,1)S(1)}, u32[]{:S(2)}, u32[]{:S(2)}) async-start(bf16[4,128,896]{2,1,0:T(8,128)(2,1)} %in_parts.1), calls=%async_computation | async-start | bytes 1835008 | tf_op jit(solution)/shard_map/all_to_all | solution.py:35
  20.4 238.2 %all-gather.7.cloned.1.call-start = ((), (), s32[]{:S(2)}) async-start(), calls=%async_computation.4 | async-start | bytes 3028992 | tf_op jit(solution)/shard_map/all_gather | solution.py:326
  20.4 26.5 %collective-permute-start.2 = (bf16[3584,128]{1,0:T(8,128)(2,1)S(1)}, bf16[3584,128]{1,0:T(8,128)(2,1)}, u32[]{:S(2)}, u32[]{:S(2)}) collective-permute-start(bf16[3584,128]{1,0:T(8,128)(2,1)S(1)} %bitcast.25), channel_id=1, source_target_pairs={{48,0},{0,16},{16,32},{32,48},{49,1},{1,17},{17,33},{33,49},{50,2}... | collective-permute-start | bytes 2752520 | tf_op jit(solution)/shard_map/ppermute | solution.py:31
  22.3 26.5 %collective-permute-start.1 = (bf16[3584,128]{1,0:T(8,128)(2,1)S(1)}, bf16[3584,128]{1,0:T(8,128)(2,1)}, u32[]{:S(2)}, u32[]{:S(2)}) collective-permute-start(bf16[3584,128]{1,0:T(8,128)(2,1)S(1)} %bitcast.29), channel_id=1, source_target_pairs={{16,0},{32,16},{48,32},{0,48},{17,1},{33,17},{49,33},{1,49},{18,2}... | collective-permute-start | bytes 2752520 | tf_op jit(solution)/shard_map/ppermute | solution.py:31
  27.4 40.4 %collective-permute-start = (bf16[3584,128]{1,0:T(8,128)(2,1)S(1)}, bf16[3584,128]{1,0:T(8,128)(2,1)S(1)}, u32[]{:S(2)}, u32[]{:S(2)}) collective-permute-start(bf16[3584,128]{1,0:T(8,128)(2,1)S(1)} %bitcast.26), channel_id=1, source_target_pairs={{16,0},{32,16},{48,32},{0,48},{17,1},{33,17},{49,33},{1,49},{18,2}... | collective-permute-start | bytes 2752520 | tf_op jit(solution)/shard_map/ppermute | solution.py:31
  29.4 39.5 %collective-permute-start.5 = (bf16[3584,128]{1,0:T(8,128)(2,1)S(1)}, bf16[3584,128]{1,0:T(8,128)(2,1)}, u32[]{:S(2)}, u32[]{:S(2)}) collective-permute-start(bf16[3584,128]{1,0:T(8,128)(2,1)S(1)} %bitcast.30), channel_id=1, source_target_pairs={{48,0},{0,16},{16,32},{32,48},{49,1},{1,17},{17,33},{33,49},{50,2}... | collective-permute-start | bytes 2752520 | tf_op jit(solution)/shard_map/ppermute | solution.py:31
  46.9 39.3 %collective-permute-start.3 = (bf16[3584,128]{1,0:T(8,128)(2,1)}, bf16[3584,128]{1,0:T(8,128)(2,1)}, u32[]{:S(2)}, u32[]{:S(2)}) collective-permute-start(bf16[3584,128]{1,0:T(8,128)(2,1)} %collective-permute-done.2.before_g), channel_id=1, source_target_pairs={{48,0},{0,16},{16,32},{32,48},{49,1},{1,17},{17,33},{33,49},{50,2}... | collective-permute-start | bytes 2752520 | tf_op jit(solution)/shard_map/ppermute | solution.py:31
  48.8 58.5 %collective-permute-start.4 = (bf16[3584,128]{1,0:T(8,128)(2,1)}, bf16[3584,128]{1,0:T(8,128)(2,1)}, u32[]{:S(2)}, u32[]{:S(2)}) collective-permute-start(bf16[3584,128]{1,0:T(8,128)(2,1)} %collective-permute-done.1.after_u), channel_id=1, source_target_pairs={{16,0},{32,16},{48,32},{0,48},{17,1},{33,17},{49,33},{1,49},{18,2}... | collective-permute-start | bytes 2752520 | tf_op jit(solution)/shard_map/ppermute | solution.py:31
  67.9 1.0 copy-start.3
  68.9 47.7 %copy-start = (bf16[4,128,896]{2,1,0:T(8,128)(2,1)}, bf16[4,128,896]{2,1,0:T(8,128)(2,1)S(1)}, u32[]{:S(2)}) copy-start(bf16[4,128,896]{2,1,0:T(8,128)(2,1)S(1)} %all-to-all-done) | copy-start | bytes 2752516
  68.9 63.3 %collective-permute-start.8 = (bf16[512,896]{1,0:T(8,128)(2,1)S(1)}, bf16[512,896]{1,0:T(8,128)(2,1)S(1)}, u32[]{:S(2)}, u32[]{:S(2)}) collective-permute-start(bf16[512,896]{1,0:T(8,128)(2,1)S(1)} %bitcast.18), channel_id=1, source_target_pairs={{48,0},{0,16},{16,32},{32,48},{49,1},{1,17},{17,33},{33,49},{50,2}... | collective-permute-start | bytes 2752520 | tf_op jit(solution)/shard_map/ppermute | solution.py:31
  70.8 61.4 %collective-permute-start.7 = (bf16[512,896]{1,0:T(8,128)(2,1)S(1)}, bf16[512,896]{1,0:T(8,128)(2,1)S(1)}, u32[]{:S(2)}, u32[]{:S(2)}) collective-permute-start(bf16[512,896]{1,0:T(8,128)(2,1)S(1)} %bitcast.19), channel_id=1, source_target_pairs={{32,0},{48,16},{0,32},{16,48},{33,1},{49,17},{1,33},{17,49},{34,2}... | collective-permute-start | bytes 2752520 | tf_op jit(solution)/shard_map/ppermute | solution.py:31
  77.8 54.4 %collective-permute-start.6 = (bf16[512,896]{1,0:T(8,128)(2,1)S(1)}, bf16[512,896]{1,0:T(8,128)(2,1)}, u32[]{:S(2)}, u32[]{:S(2)}) collective-permute-start(bf16[512,896]{1,0:T(8,128)(2,1)S(1)} %bitcast.20), channel_id=1, source_target_pairs={{16,0},{32,16},{48,32},{0,48},{17,1},{33,17},{49,33},{1,49},{18,2}... | collective-permute-start | bytes 2752520 | tf_op jit(solution)/shard_map/ppermute | solution.py:31
  132.2 0.9 copy-start.4
  132.2 1.2 copy-start.5
  180.9 2.5 collective-permute-start.9
  183.4 0.7 copy-start.6
Sparse Core Ops, SparseCore 0:
  10.1 83.7 all-gather.4
  186.1 72.5 all-gather.6

commit v5 on v4

--- a/solution.py
+++ b/solution.py
@@ -18,6 +18,7 @@
 MIB = 1 << 20
 LANES = 128
 SUBLANES = 8
+CHUNKS = 7
 
 
 def shifted(shard, axis, by):
@@ -117,6 +118,7 @@
         out_specs=(vmem, vmem),
         scratch_shapes=[pltpu.VMEM((LANES, LANES), jnp.float32)],
         cost_estimate=pl.CostEstimate(flops=6 * fed.size, bytes_accessed=8 * fed.size, transcendentals=0),
+        compiler_params=pltpu.CompilerParams(vmem_limit_bytes=8 * MIB),
         name="enter",
     )(is_first, fed, handed, gain, routes, gates)
 
@@ -166,48 +168,45 @@
 
 def up_kernel(
     capacity, block_rows, wanted_ref, tokens_ref, own_g, own_u, after_g, after_u, far_g, far_u,
-    before_g, before_u, packed_ref, place_ref, gate_ref, tokens, weights, sems, token_sem,
+    before_g, before_u, packed_ref, place_ref, gate_ref, tokens, facts, weights, total, sems, facts_sem,
 ):
-    token_copy = pltpu.make_async_copy(tokens_ref, tokens, token_sem)
-    token_copy.start()
     pieces = (own_g, own_u, after_g, after_u, far_g, far_u, before_g, before_u)
-    copies = [pltpu.make_async_copy(pieces[i], weights.at[i], sems.at[i]) for i in range(2 * QUARTERS)]
-    for copy in copies[:4]:
-        copy.start()
-    token_copy.wait()
-    rows = tokens.shape[0]
-    width = tokens.shape[1] - LANES
-    slots = packed_ref.shape[1]
-    place, gate = slot_tables(tokens[:, width:], wanted_ref, block_rows, capacity)
+    rows, width = tokens.shape
+    step = width // CHUNKS
+    facts_copy = pltpu.make_async_copy(tokens_ref.at[:, pl.ds(width, LANES)], facts, facts_sem)
+    facts_copy.start()
+    copies = []
+    for k in range(CHUNKS):
+        part = pl.ds(k * step, step)
+        group = [pltpu.make_async_copy(tokens_ref.at[:, part], tokens.at[:, part], sems.at[k, 2 * QUARTERS])]
+        for i, piece in enumerate(pieces):
+            group.append(pltpu.make_async_copy(piece.at[part], weights.at[i, part], sems.at[k, i]))
+        for copy in group:
+            copy.start()
+        copies.append(group)
+    slots, units = packed_ref.shape[1:]
+    for k in range(CHUNKS):
+        for copy in copies[k]:
+            copy.wait()
+        part = slice(k * step, (k + 1) * step)
+        wide = jnp.concatenate([weights[i, part] for i in range(2 * QUARTERS)], axis=1)
+        inner = jnp.dot(tokens[:, part], wide, preferred_element_type=jnp.float32)
+        if k == 0:
+            total[...] = inner
+        else:
+            total[...] += inner
+    facts_copy.wait()
+    place, gate = slot_tables(facts[...], wanted_ref, block_rows, capacity)
     place_ref[...] = place
     gate_ref[...] = gate
     slot = lax.broadcasted_iota(jnp.int32, (slots, rows), 0)
-    pack = jnp.concatenate(
-        [
-            jnp.where(slot == place[ahead : ahead + 1, :], 1.0, 0.0).astype(jnp.bfloat16)
-            for ahead in range(QUARTERS)
-        ],
-        axis=0,
-    )
-    sent = jnp.dot(pack, tokens[:, :width], preferred_element_type=jnp.float32).astype(jnp.bfloat16)
     for ahead in range(QUARTERS):
-        copies[2 * ahead].wait()
-        copies[2 * ahead + 1].wait()
-        if ahead < 2:
-            copies[2 * ahead + 4].start()
-            copies[2 * ahead + 5].start()
-        mine = sent[ahead * slots : (ahead + 1) * slots]
-        both = jnp.concatenate([weights[2 * ahead], weights[2 * ahead + 1]], axis=1)
-        inner = jnp.dot(
-            mine[:, : width // 2], both[: width // 2], preferred_element_type=jnp.float32
-        )
-        inner = inner + jnp.dot(
-            mine[:, width // 2 :], both[width // 2 :], preferred_element_type=jnp.float32
-        )
-        units = inner.shape[1] // 2
-        gates = inner[:, :units]
-        hidden = gates / (1.0 + jnp.exp(-gates)) * inner[:, units:]
-        packed_ref[ahead] = hidden.astype(jnp.bfloat16)
+        first = 2 * ahead * units
+        gates = total[:, first : first + units]
+        hidden = gates / (1.0 + jnp.exp(-gates)) * total[:, first + units : first + 2 * units]
+        pack = jnp.where(slot == place[ahead : ahead + 1, :], 1.0, 0.0).astype(jnp.bfloat16)
+        packed = jnp.dot(pack, hidden.astype(jnp.bfloat16), preferred_element_type=jnp.float32)
+        packed_ref[ahead] = packed.astype(jnp.bfloat16)
 
 
 def expert_up(tokens, wanted, in_w, slots, block_rows):
@@ -226,16 +225,18 @@
         in_specs=[pl.BlockSpec(memory_space=pltpu.SMEM)] + [in_hbm] * 9,
         out_specs=(vmem, vmem, vmem),
         scratch_shapes=[
-            pltpu.VMEM(tokens.shape, jnp.bfloat16),
+            pltpu.VMEM((rows, width), jnp.bfloat16),
+            pltpu.VMEM((rows, LANES), jnp.bfloat16),
             pltpu.VMEM((2 * QUARTERS, width, units), jnp.bfloat16),
-            pltpu.SemaphoreType.DMA((2 * QUARTERS,)),
+            pltpu.VMEM((rows, 2 * QUARTERS * units), jnp.float32),
+            pltpu.SemaphoreType.DMA((CHUNKS, 2 * QUARTERS + 1)),
             pltpu.SemaphoreType.DMA,
         ],
         compiler_params=pltpu.CompilerParams(vmem_limit_bytes=60 * MIB),
         cost_estimate=pl.CostEstimate(
-            flops=2 * QUARTERS * slots * width * (2 * units + rows),
+            flops=4 * QUARTERS * rows * width * units,
             bytes_accessed=2 * width * (rows + 2 * QUARTERS * units),
-            transcendentals=QUARTERS * slots * units,
+            transcendentals=QUARTERS * rows * units,
         ),
         name="expert_up",
     )(wanted, tokens, *in_w)
@@ -287,7 +288,7 @@
             pltpu.VMEM((2, QUARTERS * slots, part), jnp.bfloat16),
             pltpu.SemaphoreType.DMA((QUARTERS,)),
         ],
-        compiler_params=pltpu.CompilerParams(vmem_limit_bytes=60 * MIB),
+        compiler_params=pltpu.CompilerParams(vmem_limit_bytes=16 * MIB),
         cost_estimate=pl.CostEstimate(
             flops=2 * QUARTERS * slots * part * (units + 2 * rows),
             bytes_accessed=2 * QUARTERS * units * (part + slots),
@@ -317,6 +318,7 @@
         cost_estimate=pl.CostEstimate(
             flops=returned.size, bytes_accessed=2 * returned.size + 4 * entry.size, transcendentals=0
         ),
+        compiler_params=pltpu.CompilerParams(vmem_limit_bytes=8 * MIB),
         name="leave",
     )(entry, returned)
 

time: 333 us -> 324 us (0.973)
  the two profiles are of different devices: /device:TPU:32 before, /device:TPU:2 now
where the time goes in v5:
time: 324 us; the launch traced here: 323 us
  waiting for transfers between devices  128 us (40%)
  blocking collectives  110 us (34%)
  starting transfers between devices  39 us (12%)
  Pallas kernels  27.4 us (8%)
  between operations  14.3 us (4%)
  local copies, waits for them, and re-layouts  3.8 us (1%)
    all_to_all x2, blocking collectives, swap(): return lax.all_to_all(blocks, axis, split_axis=0, concat_axis=0, tiled=True)  79.5 us
    all_gather x2, waiting for transfers between devices, layer(): tokens = lax.all_gather(sent, RING, tiled=True)  69.3 us
    ppermute x9, waiting for transfers between devices, fetched(): lax.ppermute(shard, axis, [((i + ahead) % peers, i) for i in range(peers)])  53.8 us
    ppermute x9, starting transfers between devices, fetched(): lax.ppermute(shard, axis, [((i + ahead) % peers, i) for i in range(peers)])  31.2 us
    all_gather x2, blocking collectives, layer(): hidden = lax.all_gather(hidden, 'b', axis=0)  30.3 us
    pallas_call x2, Pallas kernels, expert_up(): pl.pallas_call(functools.partial(up_kernel, capacity, block_rows), out_sh...  14.4 us
  transfers between devices with their start and end apart: 13, of which 6 were waited for; matrix products, arithmetic and copies ran while one was open for 0% of the time, Pallas kernels for 3%

profile of v5, /device:TPU:2, one launch (start us, length us, event | category | flops | bytes accessed | tf_op | source)
XLA Modules:
  0.0 323.0 jit_solution(749780364134140025)
XLA Ops:
  7.2 0.0 copy-start.9
  7.2 0.0 copy-start.10
  7.2 0.0 all-gather.5.cloned.1.call-start
  7.2 1.9 start.1
  9.1 0.0 all-gather.5.cloned.1.call-update
  9.2 2.3 in_parts.1
  11.4 5.9 %all-to-all-start = ((bf16[4,128,896]{2,1,0:T(8,128)(2,1)}), bf16[4,128,896]{2,1,0:T(8,128)(2,1)S(1)}, u32[]{:S(2)}, u32[]{:S(2)}) async-start(bf16[4,128,896]{2,1,0:T(8,128)(2,1)} %in_parts.1), calls=%async_computation | async-start | bytes 1835008 | tf_op jit(solution)/shard_map/all_to_all | solution.py:36
  17.3 3.5 %collective-permute-start.2 = (bf16[3584,128]{1,0:T(8,128)(2,1)S(1)}, bf16[3584,128]{1,0:T(8,128)(2,1)}, u32[]{:S(2)}, u32[]{:S(2)}) collective-permute-start(bf16[3584,128]{1,0:T(8,128)(2,1)S(1)} %bitcast.38), channel_id=1, source_target_pairs={{48,0},{0,16},{16,32},{32,48},{49,1},{1,17},{17,33},{33,49},{50,2}... | collective-permute-start | bytes 2752520 | tf_op jit(solution)/shard_map/ppermute | solution.py:32
  20.8 3.6 %collective-permute-start.1 = (bf16[3584,128]{1,0:T(8,128)(2,1)S(1)}, bf16[3584,128]{1,0:T(8,128)(2,1)}, u32[]{:S(2)}, u32[]{:S(2)}) collective-permute-start(bf16[3584,128]{1,0:T(8,128)(2,1)S(1)} %bitcast.42), channel_id=1, source_target_pairs={{16,0},{32,16},{48,32},{0,48},{17,1},{33,17},{49,33},{1,49},{18,2}... | collective-permute-start | bytes 2752520 | tf_op jit(solution)/shard_map/ppermute | solution.py:32
  24.4 3.7 %collective-permute-start = (bf16[3584,128]{1,0:T(8,128)(2,1)S(1)}, bf16[3584,128]{1,0:T(8,128)(2,1)S(1)}, u32[]{:S(2)}, u32[]{:S(2)}) collective-permute-start(bf16[3584,128]{1,0:T(8,128)(2,1)S(1)} %bitcast.39), channel_id=1, source_target_pairs={{16,0},{32,16},{48,32},{0,48},{17,1},{33,17},{49,33},{1,49},{18,2}... | collective-permute-start | bytes 2752520 | tf_op jit(solution)/shard_map/ppermute | solution.py:32
  28.1 2.1 collective-permute-start.5
  30.3 13.5 %collective-permute-done.2.before_g = bf16[3584,128]{1,0:T(8,128)(2,1)} collective-permute-done((bf16[3584,128]{1,0:T(8,128)(2,1)S(1)}, bf16[3584,128]{1,0:T(8,128)(2,1)}, u32[]{:S(2)}, u32[]{:S(2)}) %collective-permute-start.2) | collective-permute-done | bytes 917536 | tf_op jit(solution)/shard_map/ppermute | solution.py:32
  43.8 2.3 collective-permute-start.3
  46.1 0.0 collective-permute-done.1.after_u
  46.1 4.8 %collective-permute-start.4 = (bf16[3584,128]{1,0:T(8,128)(2,1)}, bf16[3584,128]{1,0:T(8,128)(2,1)}, u32[]{:S(2)}, u32[]{:S(2)}) collective-permute-start(bf16[3584,128]{1,0:T(8,128)(2,1)} %collective-permute-done.1.after_u), channel_id=1, source_target_pairs={{16,0},{32,16},{48,32},{0,48},{17,1},{33,17},{49,33},{1,49},{18,2}... | collective-permute-start | bytes 2752520 | tf_op jit(solution)/shard_map/ppermute | solution.py:32
  50.9 14.8 %collective-permute-done.after_g = bf16[3584,128]{1,0:T(8,128)(2,1)S(1)} collective-permute-done((bf16[3584,128]{1,0:T(8,128)(2,1)S(1)}, bf16[3584,128]{1,0:T(8,128)(2,1)S(1)}, u32[]{:S(2)}, u32[]{:S(2)}) %collective-permute-start) | collective-permute-done | bytes 917536 | tf_op jit(solution)/shard_map/ppermute | solution.py:32
  65.7 0.9 copy-done.11
  66.6 0.0 collective-permute-done.5.before_u
  66.6 0.0 all-to-all-done
  66.6 3.5 %collective-permute-start.8 = (bf16[512,896]{1,0:T(8,128)(2,1)S(1)}, bf16[512,896]{1,0:T(8,128)(2,1)S(1)}, u32[]{:S(2)}, u32[]{:S(2)}) collective-permute-start(bf16[512,896]{1,0:T(8,128)(2,1)S(1)} %bitcast.18), channel_id=1, source_target_pairs={{48,0},{0,16},{16,32},{32,48},{49,1},{1,17},{17,33},{33,49},{50,2}... | collective-permute-start | bytes 2752520 | tf_op jit(solution)/shard_map/ppermute | solution.py:32
  70.1 4.7 %collective-permute-start.7 = (bf16[512,896]{1,0:T(8,128)(2,1)S(1)}, bf16[512,896]{1,0:T(8,128)(2,1)S(1)}, u32[]{:S(2)}, u32[]{:S(2)}) collective-permute-start(bf16[512,896]{1,0:T(8,128)(2,1)S(1)} %bitcast.19), channel_id=1, source_target_pairs={{32,0},{48,16},{0,32},{16,48},{33,1},{49,17},{1,33},{17,49},{34,2}... | collective-permute-start | bytes 2752520 | tf_op jit(solution)/shard_map/ppermute | solution.py:32
  74.8 3.1 collective-permute-start.6
  77.9 0.6 fusion.1.wanted_ref
  78.5 4.6 %collective-permute-done.3.far_g = bf16[3584,128]{1,0:T(8,128)(2,1)} collective-permute-done((bf16[3584,128]{1,0:T(8,128)(2,1)}, bf16[3584,128]{1,0:T(8,128)(2,1)}, u32[]{:S(2)}, u32[]{:S(2)}) %collective-permute-start.3) | collective-permute-done | bytes 917536 | tf_op jit(solution)/shard_map/ppermute | solution.py:32
  83.1 20.8 %collective-permute-done.4.far_u = bf16[3584,128]{1,0:T(8,128)(2,1)} collective-permute-done((bf16[3584,128]{1,0:T(8,128)(2,1)}, bf16[3584,128]{1,0:T(8,128)(2,1)}, u32[]{:S(2)}, u32[]{:S(2)}) %collective-permute-start.4) | collective-permute-done | bytes 917536 | tf_op jit(solution)/shard_map/ppermute | solution.py:32
  103.9 7.2 %expert_up.2 = (bf16[4,128,128]{2,1,0:T(8,128)(2,1)}, s32[8,384]{1,0:T(8,128)}, f32[8,384]{1,0:T(8,128)}) custom-call(s32[4]{0:T(128)} %fusion.1.wanted_ref, bf16[384,3712]{1,0:T(8,128)(2,1)} %all-gather.5.cloned.1.call-done.tokens_ref, bf16[3584,128]{1,0:T(8,128)(2,1)} %bitcast.36, bf16[3584,128]{1,0:T(8,128)(2,1)} %bitcast.40, ...), custom_call_target="tpu_custom_call" | custom-call | flops 2818572288 | bytes 10092544 | tf_op jit(solution)/shard_map/expert_up/pallas_call | solution.py:218
  111.2 15.4 %all-gather = bf16[16,128,128]{2,1,0:T(8,128)(2,1)S(1)} all-gather(bf16[4,128,128]{2,1,0:T(8,128)(2,1)} %get-tuple-element.11), channel_id=2, replica_groups=mesh['section'=8,'y'=4,'q'=4,'b'=4] {'b'}, dimensions={0}, use_global_device_ids=true | all-gather | bytes 655360 | tf_op jit(solution)/shard_map/all_gather | solution.py:330
  126.6 0.0 collective-permute-done.8.before
  126.6 0.0 collective-permute-done.7.far
  126.6 0.0 copy-start.5
  126.6 0.7 copy-done.5
  127.3 0.7 copy-done.6
  128.1 0.0 copy-start.8
  128.1 3.2 expert_down.2
  131.3 46.2 %all_to_all.15.returned_ref = bf16[16,24,896]{2,1,0:T(8,128)(2,1)S(1)} all-to-all(bf16[16,24,896]{2,1,0:T(8,128)(2,1)S(1)} %bitcast.24), channel_id=1, replica_groups=mesh['section'=8,'y'=4,'q'=4,'b'=4] {'q','b'}, dimensions={0} | all-to-all | bytes 1376256 | tf_op jit(solution)/shard_map/all_to_all | solution.py:36
  177.5 0.8 leave.2
  178.3 1.9 collective-permute-start.9
  180.2 5.0 %collective-permute-done.9.handed_ref = bf16[24,3584]{1,0:T(8,128)(2,1)S(1)} collective-permute-done((bf16[24,3584]{1,0:T(8,128)(2,1)}, bf16[24,3584]{1,0:T(8,128)(2,1)S(1)}, u32[]{:S(2)}, u32[]{:S(2)}) %collective-permute-start.9) | collective-permute-done | bytes 172064 | tf_op jit(solution)/shard_map/ppermute | solution.py:27
  185.3 0.8 enter.1
  186.1 0.0 all-gather.7.cloned.1.call-update
  186.1 69.3 %all-gather.7.cloned.1.call-done.tokens_ref = bf16[384,3712]{1,0:T(8,128)(2,1)} async-done(((bf16[24,3712]{1,0:T(8,128)(2,1)}), bf16[384,3712]{1,0:T(8,128)(2,1)}) %all-gather.7.cloned.1.call-update) | async-done | bytes 2850832 | tf_op jit(solution)/shard_map/all_gather | solution.py:328
  255.4 7.2 %expert_up.3 = (bf16[4,128,128]{2,1,0:T(8,128)(2,1)}, s32[8,384]{1,0:T(8,128)}, f32[8,384]{1,0:T(8,128)}) custom-call(s32[4]{0:T(128)} %fusion.1.wanted_ref, bf16[384,3712]{1,0:T(8,128)(2,1)} %all-gather.7.cloned.1.call-done.tokens_ref, bf16[3584,128]{1,0:T(8,128)(2,1)} %bitcast.37, bf16[3584,128]{1,0:T(8,128)(2,1)} %bitcast.41, ...), custom_call_target="tpu_custom_call" | custom-call | flops 2818572288 | bytes 10092544 | tf_op jit(solution)/shard_map/expert_up/pallas_call | solution.py:218
  262.6 14.9 %all-gather.1 = bf16[16,128,128]{2,1,0:T(8,128)(2,1)S(1)} all-gather(bf16[4,128,128]{2,1,0:T(8,128)(2,1)} %get-tuple-element.17), channel_id=3, replica_groups=mesh['section'=8,'y'=4,'q'=4,'b'=4] {'b'}, dimensions={0}, use_global_device_ids=true | all-gather | bytes 655360 | tf_op jit(solution)/shard_map/all_gather | solution.py:330
  277.5 0.7 copy-done.3
  278.2 0.7 copy-done.4
  278.9 3.2 expert_down.3
  282.1 33.3 %all_to_all.16.returned_ref = bf16[16,24,896]{2,1,0:T(8,128)(2,1)S(1)} all-to-all(bf16[16,24,896]{2,1,0:T(8,128)(2,1)S(1)} %bitcast.23), channel_id=1, replica_groups=mesh['section'=8,'y'=4,'q'=4,'b'=4] {'q','b'}, dimensions={0} | all-to-all | bytes 1376256 | tf_op jit(solution)/shard_map/all_to_all | solution.py:36
  315.4 0.8 leave.3
  (18 shorter events, 0.0 us)
Async XLA Ops:
  7.2 10.2 %copy-start.9 = (bf16[1,3584,128]{2,1,0:T(8,128)(2,1)S(1)}, bf16[1,3584,128]{2,1,0:T(8,128)(2,1)}, u32[]{:S(2)}) copy-start(bf16[1,3584,128]{2,1,0:T(8,128)(2,1)} %param.13) | copy-start | bytes 2752516
  7.2 13.7 %copy-start.10 = (bf16[1,3584,128]{2,1,0:T(8,128)(2,1)S(1)}, bf16[1,3584,128]{2,1,0:T(8,128)(2,1)}, u32[]{:S(2)}) copy-start(bf16[1,3584,128]{2,1,0:T(8,128)(2,1)} %param.14) | copy-start | bytes 2752516
  7.2 96.8 %all-gather.5.cloned.1.call-start = ((), (), s32[]{:S(2)}) async-start(), calls=%async_computation.3 | async-start | bytes 3028992 | tf_op jit(solution)/shard_map/all_gather | solution.py:328
  11.4 55.2 %all-to-all-start = ((bf16[4,128,896]{2,1,0:T(8,128)(2,1)}), bf16[4,128,896]{2,1,0:T(8,128)(2,1)S(1)}, u32[]{:S(2)}, u32[]{:S(2)}) async-start(bf16[4,128,896]{2,1,0:T(8,128)(2,1)} %in_parts.1), calls=%async_computation | async-start | bytes 1835008 | tf_op jit(solution)/shard_map/all_to_all | solution.py:36
  17.3 238.1 %all-gather.7.cloned.1.call-start = ((), (), s32[]{:S(2)}) async-start(), calls=%async_computation.4 | async-start | bytes 3028992 | tf_op jit(solution)/shard_map/all_gather | solution.py:328
  17.3 26.5 %collective-permute-start.2 = (bf16[3584,128]{1,0:T(8,128)(2,1)S(1)}, bf16[3584,128]{1,0:T(8,128)(2,1)}, u32[]{:S(2)}, u32[]{:S(2)}) collective-permute-start(bf16[3584,128]{1,0:T(8,128)(2,1)S(1)} %bitcast.38), channel_id=1, source_target_pairs={{48,0},{0,16},{16,32},{32,48},{49,1},{1,17},{17,33},{33,49},{50,2}... | collective-permute-start | bytes 2752520 | tf_op jit(solution)/shard_map/ppermute | solution.py:32
  20.8 25.3 %collective-permute-start.1 = (bf16[3584,128]{1,0:T(8,128)(2,1)S(1)}, bf16[3584,128]{1,0:T(8,128)(2,1)}, u32[]{:S(2)}, u32[]{:S(2)}) collective-permute-start(bf16[3584,128]{1,0:T(8,128)(2,1)S(1)} %bitcast.42), channel_id=1, source_target_pairs={{16,0},{32,16},{48,32},{0,48},{17,1},{33,17},{49,33},{1,49},{18,2}... | collective-permute-start | bytes 2752520 | tf_op jit(solution)/shard_map/ppermute | solution.py:32
  24.4 41.3 %collective-permute-start = (bf16[3584,128]{1,0:T(8,128)(2,1)S(1)}, bf16[3584,128]{1,0:T(8,128)(2,1)S(1)}, u32[]{:S(2)}, u32[]{:S(2)}) collective-permute-start(bf16[3584,128]{1,0:T(8,128)(2,1)S(1)} %bitcast.39), channel_id=1, source_target_pairs={{16,0},{32,16},{48,32},{0,48},{17,1},{33,17},{49,33},{1,49},{18,2}... | collective-permute-start | bytes 2752520 | tf_op jit(solution)/shard_map/ppermute | solution.py:32
  28.1 38.5 %collective-permute-start.5 = (bf16[3584,128]{1,0:T(8,128)(2,1)S(1)}, bf16[3584,128]{1,0:T(8,128)(2,1)}, u32[]{:S(2)}, u32[]{:S(2)}) collective-permute-start(bf16[3584,128]{1,0:T(8,128)(2,1)S(1)} %bitcast.43), channel_id=1, source_target_pairs={{48,0},{0,16},{16,32},{32,48},{49,1},{1,17},{17,33},{33,49},{50,2}... | collective-permute-start | bytes 2752520 | tf_op jit(solution)/shard_map/ppermute | solution.py:32
  43.8 39.3 %collective-permute-start.3 = (bf16[3584,128]{1,0:T(8,128)(2,1)}, bf16[3584,128]{1,0:T(8,128)(2,1)}, u32[]{:S(2)}, u32[]{:S(2)}) collective-permute-start(bf16[3584,128]{1,0:T(8,128)(2,1)} %collective-permute-done.2.before_g), channel_id=1, source_target_pairs={{48,0},{0,16},{16,32},{32,48},{49,1},{1,17},{17,33},{33,49},{50,2}... | collective-permute-start | bytes 2752520 | tf_op jit(solution)/shard_map/ppermute | solution.py:32
  46.1 57.8 %collective-permute-start.4 = (bf16[3584,128]{1,0:T(8,128)(2,1)}, bf16[3584,128]{1,0:T(8,128)(2,1)}, u32[]{:S(2)}, u32[]{:S(2)}) collective-permute-start(bf16[3584,128]{1,0:T(8,128)(2,1)} %collective-permute-done.1.after_u), channel_id=1, source_target_pairs={{16,0},{32,16},{48,32},{0,48},{17,1},{33,17},{49,33},{1,49},{18,2}... | collective-permute-start | bytes 2752520 | tf_op jit(solution)/shard_map/ppermute | solution.py:32
  65.7 0.9 copy-start.11
  66.6 60.0 %collective-permute-start.8 = (bf16[512,896]{1,0:T(8,128)(2,1)S(1)}, bf16[512,896]{1,0:T(8,128)(2,1)S(1)}, u32[]{:S(2)}, u32[]{:S(2)}) collective-permute-start(bf16[512,896]{1,0:T(8,128)(2,1)S(1)} %bitcast.18), channel_id=1, source_target_pairs={{48,0},{0,16},{16,32},{32,48},{49,1},{1,17},{17,33},{33,49},{50,2}... | collective-permute-start | bytes 2752520 | tf_op jit(solution)/shard_map/ppermute | solution.py:32
  70.1 56.5 %collective-permute-start.7 = (bf16[512,896]{1,0:T(8,128)(2,1)S(1)}, bf16[512,896]{1,0:T(8,128)(2,1)S(1)}, u32[]{:S(2)}, u32[]{:S(2)}) collective-permute-start(bf16[512,896]{1,0:T(8,128)(2,1)S(1)} %bitcast.19), channel_id=1, source_target_pairs={{32,0},{48,16},{0,32},{16,48},{33,1},{49,17},{1,33},{17,49},{34,2}... | collective-permute-start | bytes 2752520 | tf_op jit(solution)/shard_map/ppermute | solution.py:32
  74.8 51.8 %collective-permute-start.6 = (bf16[512,896]{1,0:T(8,128)(2,1)S(1)}, bf16[512,896]{1,0:T(8,128)(2,1)}, u32[]{:S(2)}, u32[]{:S(2)}) collective-permute-start(bf16[512,896]{1,0:T(8,128)(2,1)S(1)} %bitcast.20), channel_id=1, source_target_pairs={{16,0},{32,16},{48,32},{0,48},{17,1},{33,17},{49,33},{1,49},{18,2}... | collective-permute-start | bytes 2752520 | tf_op jit(solution)/shard_map/ppermute | solution.py:32
  126.6 0.7 copy-start.5
  127.3 0.7 copy-start.6
  128.1 49.5 %copy-start = (bf16[1,24,3584]{2,1,0:T(8,128)(2,1)S(1)}, bf16[1,24,3584]{2,1,0:T(8,128)(2,1)}, u32[]{:S(2)}) copy-start(bf16[1,24,3584]{2,1,0:T(8,128)(2,1)} %param.8) | copy-start | bytes 516100
  128.1 57.2 %copy-start.1 = (bf16[24,3584]{1,0:T(8,128)(2,1)S(1)}, bf16[24,3584]{1,0:T(8,128)(2,1)}, u32[]{:S(2)}) copy-start(bf16[24,3584]{1,0:T(8,128)(2,1)} %fed_ref.1) | copy-start | bytes 516100
  128.1 57.2 %copy-start.2 = (f32[1,3584]{1,0:T(1,128)S(1)}, f32[1,3584]{1,0:T(1,128)}, u32[]{:S(2)}) copy-start(f32[1,3584]{1,0:T(1,128)} %gain_ref.3) | copy-start | bytes 43012
  128.1 57.2 %copy-start.7 = (s32[2,1,24,2]{2,3,1,0:T(2,128)S(1)}, s32[2,1,24,2]{2,3,1,0:T(2,128)}, u32[]{:S(2)}) copy-start(s32[2,1,24,2]{2,3,1,0:T(2,128)} %param.10) | copy-start | bytes 1156
  128.1 57.2 %copy-start.8 = (f32[2,1,24,2]{2,3,1,0:T(2,128)S(1)}, f32[2,1,24,2]{2,3,1,0:T(2,128)}, u32[]{:S(2)}) copy-start(f32[2,1,24,2]{2,3,1,0:T(2,128)} %param.11) | copy-start | bytes 1156
  178.3 6.9 %collective-permute-start.9 = (bf16[24,3584]{1,0:T(8,128)(2,1)}, bf16[24,3584]{1,0:T(8,128)(2,1)S(1)}, u32[]{:S(2)}, u32[]{:S(2)}) collective-permute-start(bf16[24,3584]{1,0:T(8,128)(2,1)} %leave.2), channel_id=1, source_target_pairs={{0,64},{64,128},{128,192},{192,256},{256,320},{320,384},{384,448},... | collective-permute-start | bytes 516104 | tf_op jit(solution)/shard_map/ppermute | solution.py:27
  277.5 0.7 copy-start.3
  278.2 0.7 copy-start.4
Sparse Core Ops, SparseCore 0:
  10.1 84.8 all-gather.4
  186.3 69.0 all-gather.6

commit v6 on v5

--- a/solution.py
+++ b/solution.py
@@ -356,7 +356,10 @@
     in_w = (gate_w, up_w, after_gate, after_up, far_gate, far_up, before_gate, before_up)
     out_w = swap(parted, "b").reshape(-1, part)
     out_w, _, _ = lax.optimization_barrier((out_w, after_gate, before_up))
-    out_w = (out_w,) + tuple(fetched(out_w, "y", ahead) for ahead in (1, 2, 3))
+    out_after, out_before = fetched(out_w, "y", 1), fetched(out_w, "y", 3)
+    far_w, far_gate, far_up = lax.optimization_barrier((out_w, far_gate, far_up))
+    in_w = (gate_w, up_w, after_gate, after_up, far_gate, far_up, before_gate, before_up)
+    out_w = (out_w, out_after, fetched(far_w, "y", 2), out_before)
     ring_place = lax.axis_index(RING)
     y_place = (lax.axis_index("y") + jnp.arange(QUARTERS, dtype=jnp.int32)) % QUARTERS
     wanted = y_place * (ring // HS) + ring_place // HS

time: 324 us -> 323 us (level)
  the two profiles are of different devices: /device:TPU:2 before, /device:TPU:32 now
where the time goes in v6:
time: 323 us; the launch traced here: 322 us
  waiting for transfers between devices  122 us (38%)
  blocking collectives  113 us (35%)
  starting transfers between devices  41.6 us (13%)
  Pallas kernels  27.2 us (8%)
  between operations  14.2 us (4%)
  local copies, waits for them, and re-layouts  3.8 us (1%)
    all_to_all x2, blocking collectives, swap(): return lax.all_to_all(blocks, axis, split_axis=0, concat_axis=0, tiled=True)  84.5 us
    all_gather x2, waiting for transfers between devices, layer(): tokens = lax.all_gather(sent, RING, tiled=True)  75.7 us
    ppermute x9, waiting for transfers between devices, fetched(): lax.ppermute(shard, axis, [((i + ahead) % peers, i) for i in range(peers)])  45.2 us
    ppermute x9, starting transfers between devices, fetched(): lax.ppermute(shard, axis, [((i + ahead) % peers, i) for i in range(peers)])  31.3 us
    all_gather x2, blocking collectives, layer(): hidden = lax.all_gather(hidden, 'b', axis=0)  28.4 us
    pallas_call x2, Pallas kernels, expert_up(): pl.pallas_call(functools.partial(up_kernel, capacity, block_rows), out_sh...  14.4 us
    all_to_all x1, starting transfers between devices, swap(): return lax.all_to_all(blocks, axis, split_axis=0, concat_axis=0, tiled=True)  8.97 us
  transfers between devices with their start and end apart: 13, of which 8 were waited for; matrix products, arithmetic and copies ran while one was open for 0% of the time, Pallas kernels for 3%

profile of v6, /device:TPU:32, one launch (start us, length us, event | category | flops | bytes accessed | tf_op | source)
XLA Modules:
  0.0 322.4 jit_solution(3584961500737502737)
XLA Ops:
  7.2 0.0 copy-start.9
  7.2 0.0 copy-start.10
  7.2 0.0 all-gather.5.cloned.1.call-start
  7.2 1.9 start.1
  9.1 0.0 all-gather.5.cloned.1.call-update
  9.2 2.3 in_parts.1
  11.4 9.0 %all-to-all-start = ((bf16[4,128,896]{2,1,0:T(8,128)(2,1)}), bf16[4,128,896]{2,1,0:T(8,128)(2,1)S(1)}, u32[]{:S(2)}, u32[]{:S(2)}) async-start(bf16[4,128,896]{2,1,0:T(8,128)(2,1)} %in_parts.1), calls=%async_computation | async-start | bytes 1835008 | tf_op jit(solution)/shard_map/all_to_all | solution.py:36
  20.4 1.9 collective-permute-start.3
  22.3 5.1 %collective-permute-start.1 = (bf16[3584,128]{1,0:T(8,128)(2,1)S(1)}, bf16[3584,128]{1,0:T(8,128)(2,1)}, u32[]{:S(2)}, u32[]{:S(2)}) collective-permute-start(bf16[3584,128]{1,0:T(8,128)(2,1)S(1)} %bitcast.42), channel_id=1, source_target_pairs={{16,0},{32,16},{48,32},{0,48},{17,1},{33,17},{49,33},{1,49},{18,2}... | collective-permute-start | bytes 2752520 | tf_op jit(solution)/shard_map/ppermute | solution.py:32
  27.5 1.9 collective-permute-start
  29.4 3.9 %collective-permute-start.2 = (bf16[3584,128]{1,0:T(8,128)(2,1)S(1)}, bf16[3584,128]{1,0:T(8,128)(2,1)}, u32[]{:S(2)}, u32[]{:S(2)}) collective-permute-start(bf16[3584,128]{1,0:T(8,128)(2,1)S(1)} %bitcast.43), channel_id=1, source_target_pairs={{48,0},{0,16},{16,32},{32,48},{49,1},{1,17},{17,33},{33,49},{50,2}... | collective-permute-start | bytes 2752520 | tf_op jit(solution)/shard_map/ppermute | solution.py:32
  33.3 13.6 %collective-permute-done.3.before_g = bf16[3584,128]{1,0:T(8,128)(2,1)} collective-permute-done((bf16[3584,128]{1,0:T(8,128)(2,1)S(1)}, bf16[3584,128]{1,0:T(8,128)(2,1)}, u32[]{:S(2)}, u32[]{:S(2)}) %collective-permute-start.3) | collective-permute-done | bytes 917536 | tf_op jit(solution)/shard_map/ppermute | solution.py:32
  46.9 1.9 collective-permute-start.4
  48.8 0.0 collective-permute-done.1.after_u
  48.8 5.1 %collective-permute-start.5 = (bf16[3584,128]{1,0:T(8,128)(2,1)}, bf16[3584,128]{1,0:T(8,128)(2,1)}, u32[]{:S(2)}, u32[]{:S(2)}) collective-permute-start(bf16[3584,128]{1,0:T(8,128)(2,1)} %collective-permute-done.1.after_u), channel_id=1, source_target_pairs={{16,0},{32,16},{48,32},{0,48},{17,1},{33,17},{49,33},{1,49},{18,2}... | collective-permute-start | bytes 2752520 | tf_op jit(solution)/shard_map/ppermute | solution.py:32
  54.0 14.0 %collective-permute-done.after_g = bf16[3584,128]{1,0:T(8,128)(2,1)S(1)} collective-permute-done((bf16[3584,128]{1,0:T(8,128)(2,1)S(1)}, bf16[3584,128]{1,0:T(8,128)(2,1)S(1)}, u32[]{:S(2)}, u32[]{:S(2)}) %collective-permute-start) | collective-permute-done | bytes 917536 | tf_op jit(solution)/shard_map/ppermute | solution.py:32
  67.9 0.9 copy-done.11
  68.9 0.0 collective-permute-done.2.before_u
  68.9 0.0 all-to-all-done
  68.9 1.9 collective-permute-start.8
  70.8 5.6 %collective-permute-start.6 = (bf16[512,896]{1,0:T(8,128)(2,1)S(1)}, bf16[512,896]{1,0:T(8,128)(2,1)S(1)}, u32[]{:S(2)}, u32[]{:S(2)}) collective-permute-start(bf16[512,896]{1,0:T(8,128)(2,1)S(1)} %bitcast.19), channel_id=1, source_target_pairs={{16,0},{32,16},{48,32},{0,48},{17,1},{33,17},{49,33},{1,49},{18,2}... | collective-permute-start | bytes 2752520 | tf_op jit(solution)/shard_map/ppermute | solution.py:32
  76.4 9.8 %collective-permute-done.4.far_g = bf16[3584,128]{1,0:T(8,128)(2,1)} collective-permute-done((bf16[3584,128]{1,0:T(8,128)(2,1)}, bf16[3584,128]{1,0:T(8,128)(2,1)}, u32[]{:S(2)}, u32[]{:S(2)}) %collective-permute-start.4) | collective-permute-done | bytes 917536 | tf_op jit(solution)/shard_map/ppermute | solution.py:32
  86.2 1.5 collective-permute-done.5.far_u
  87.7 3.8 %collective-permute-start.7 = (bf16[512,896]{1,0:T(8,128)(2,1)S(1)}, bf16[512,896]{1,0:T(8,128)(2,1)}, u32[]{:S(2)}, u32[]{:S(2)}) collective-permute-start(bf16[512,896]{1,0:T(8,128)(2,1)S(1)} %bitcast.20), channel_id=1, source_target_pairs={{32,0},{48,16},{0,32},{16,48},{33,1},{49,17},{1,33},{17,49},{34,2}... | collective-permute-start | bytes 2752520 | tf_op jit(solution)/shard_map/ppermute | solution.py:32
  91.5 0.6 fusion.1.wanted_ref
  92.1 1.7 all-gather.5.cloned.1.call-done.tokens_ref
  93.9 7.2 %expert_up.2 = (bf16[4,128,128]{2,1,0:T(8,128)(2,1)}, s32[8,384]{1,0:T(8,128)}, f32[8,384]{1,0:T(8,128)}) custom-call(s32[4]{0:T(128)} %fusion.1.wanted_ref, bf16[384,3712]{1,0:T(8,128)(2,1)} %all-gather.5.cloned.1.call-done.tokens_ref, bf16[3584,128]{1,0:T(8,128)(2,1)} %bitcast.36, bf16[3584,128]{1,0:T(8,128)(2,1)} %bitcast.40, ...), custom_call_target="tpu_custom_call" | custom-call | flops 2818572288 | bytes 10092544 | tf_op jit(solution)/shard_map/expert_up/pallas_call | solution.py:218
  101.1 14.5 %all-gather = bf16[16,128,128]{2,1,0:T(8,128)(2,1)S(1)} all-gather(bf16[4,128,128]{2,1,0:T(8,128)(2,1)} %get-tuple-element.17), channel_id=2, replica_groups=mesh['section'=8,'y'=4,'q'=4,'b'=4] {'b'}, dimensions={0}, use_global_device_ids=true | all-gather | bytes 655360 | tf_op jit(solution)/shard_map/all_gather | solution.py:330
  115.6 0.0 collective-permute-done.8.before
  115.7 6.4 %collective-permute-done.7.far = bf16[512,896]{1,0:T(8,128)(2,1)} collective-permute-done((bf16[512,896]{1,0:T(8,128)(2,1)S(1)}, bf16[512,896]{1,0:T(8,128)(2,1)}, u32[]{:S(2)}, u32[]{:S(2)}) %collective-permute-start.7) | collective-permute-done | bytes 917536 | tf_op jit(solution)/shard_map/ppermute | solution.py:32
  122.1 0.7 copy-done.5
  122.8 0.7 copy-done.6
  123.5 0.0 copy-start.8
  123.5 3.1 expert_down.2
  126.6 49.7 %all_to_all.15.returned_ref = bf16[16,24,896]{2,1,0:T(8,128)(2,1)S(1)} all-to-all(bf16[16,24,896]{2,1,0:T(8,128)(2,1)S(1)} %bitcast.24), channel_id=1, replica_groups=mesh['section'=8,'y'=4,'q'=4,'b'=4] {'q','b'}, dimensions={0} | all-to-all | bytes 1376256 | tf_op jit(solution)/shard_map/all_to_all | solution.py:36
  176.4 0.8 leave.2
  177.1 1.3 collective-permute-start.9
  178.4 1.2 collective-permute-done.9.handed_ref
  179.7 0.8 enter.1
  180.5 0.0 all-gather.7.cloned.1.call-update
  180.5 73.9 %all-gather.7.cloned.1.call-done.tokens_ref = bf16[384,3712]{1,0:T(8,128)(2,1)} async-done(((bf16[24,3712]{1,0:T(8,128)(2,1)}), bf16[384,3712]{1,0:T(8,128)(2,1)}) %all-gather.7.cloned.1.call-update) | async-done | bytes 2850832 | tf_op jit(solution)/shard_map/all_gather | solution.py:328
  254.5 7.2 %expert_up.3 = (bf16[4,128,128]{2,1,0:T(8,128)(2,1)}, s32[8,384]{1,0:T(8,128)}, f32[8,384]{1,0:T(8,128)}) custom-call(s32[4]{0:T(128)} %fusion.1.wanted_ref, bf16[384,3712]{1,0:T(8,128)(2,1)} %all-gather.7.cloned.1.call-done.tokens_ref, bf16[3584,128]{1,0:T(8,128)(2,1)} %bitcast.37, bf16[3584,128]{1,0:T(8,128)(2,1)} %bitcast.41, ...), custom_call_target="tpu_custom_call" | custom-call | flops 2818572288 | bytes 10092544 | tf_op jit(solution)/shard_map/expert_up/pallas_call | solution.py:218
  261.7 13.8 %all-gather.1 = bf16[16,128,128]{2,1,0:T(8,128)(2,1)S(1)} all-gather(bf16[4,128,128]{2,1,0:T(8,128)(2,1)} %get-tuple-element.23), channel_id=3, replica_groups=mesh['section'=8,'y'=4,'q'=4,'b'=4] {'b'}, dimensions={0}, use_global_device_ids=true | all-gather | bytes 655360 | tf_op jit(solution)/shard_map/all_gather | solution.py:330
  275.6 0.7 copy-done.3
  276.3 0.7 copy-done.4
  277.0 3.1 expert_down.3
  280.1 34.7 %all_to_all.16.returned_ref = bf16[16,24,896]{2,1,0:T(8,128)(2,1)S(1)} all-to-all(bf16[16,24,896]{2,1,0:T(8,128)(2,1)S(1)} %bitcast.23), channel_id=1, replica_groups=mesh['section'=8,'y'=4,'q'=4,'b'=4] {'q','b'}, dimensions={0} | all-to-all | bytes 1376256 | tf_op jit(solution)/shard_map/all_to_all | solution.py:36
  314.8 0.8 leave.3
  (18 shorter events, 0.0 us)
Async XLA Ops:
  7.2 13.2 %copy-start.9 = (bf16[1,3584,128]{2,1,0:T(8,128)(2,1)S(1)}, bf16[1,3584,128]{2,1,0:T(8,128)(2,1)}, u32[]{:S(2)}) copy-start(bf16[1,3584,128]{2,1,0:T(8,128)(2,1)} %param.13) | copy-start | bytes 2752516
  7.2 15.1 %copy-start.10 = (bf16[1,3584,128]{2,1,0:T(8,128)(2,1)S(1)}, bf16[1,3584,128]{2,1,0:T(8,128)(2,1)}, u32[]{:S(2)}) copy-start(bf16[1,3584,128]{2,1,0:T(8,128)(2,1)} %param.14) | copy-start | bytes 2752516
  7.2 86.7 %all-gather.5.cloned.1.call-start = ((), (), s32[]{:S(2)}) async-start(), calls=%async_computation.3 | async-start | bytes 3028992 | tf_op jit(solution)/shard_map/all_gather | solution.py:328
  11.4 57.4 %all-to-all-start = ((bf16[4,128,896]{2,1,0:T(8,128)(2,1)}), bf16[4,128,896]{2,1,0:T(8,128)(2,1)S(1)}, u32[]{:S(2)}, u32[]{:S(2)}) async-start(bf16[4,128,896]{2,1,0:T(8,128)(2,1)} %in_parts.1), calls=%async_computation | async-start | bytes 1835008 | tf_op jit(solution)/shard_map/all_to_all | solution.py:36
  20.4 234.1 %all-gather.7.cloned.1.call-start = ((), (), s32[]{:S(2)}) async-start(), calls=%async_computation.4 | async-start | bytes 3028992 | tf_op jit(solution)/shard_map/all_gather | solution.py:328
  20.4 26.5 %collective-permute-start.3 = (bf16[3584,128]{1,0:T(8,128)(2,1)S(1)}, bf16[3584,128]{1,0:T(8,128)(2,1)}, u32[]{:S(2)}, u32[]{:S(2)}) collective-permute-start(bf16[3584,128]{1,0:T(8,128)(2,1)S(1)} %bitcast.38), channel_id=1, source_target_pairs={{48,0},{0,16},{16,32},{32,48},{49,1},{1,17},{17,33},{33,49},{50,2}... | collective-permute-start | bytes 2752520 | tf_op jit(solution)/shard_map/ppermute | solution.py:32
  22.3 26.5 %collective-permute-start.1 = (bf16[3584,128]{1,0:T(8,128)(2,1)S(1)}, bf16[3584,128]{1,0:T(8,128)(2,1)}, u32[]{:S(2)}, u32[]{:S(2)}) collective-permute-start(bf16[3584,128]{1,0:T(8,128)(2,1)S(1)} %bitcast.42), channel_id=1, source_target_pairs={{16,0},{32,16},{48,32},{0,48},{17,1},{33,17},{49,33},{1,49},{18,2}... | collective-permute-start | bytes 2752520 | tf_op jit(solution)/shard_map/ppermute | solution.py:32
  27.5 40.4 %collective-permute-start = (bf16[3584,128]{1,0:T(8,128)(2,1)S(1)}, bf16[3584,128]{1,0:T(8,128)(2,1)S(1)}, u32[]{:S(2)}, u32[]{:S(2)}) collective-permute-start(bf16[3584,128]{1,0:T(8,128)(2,1)S(1)} %bitcast.39), channel_id=1, source_target_pairs={{16,0},{32,16},{48,32},{0,48},{17,1},{33,17},{49,33},{1,49},{18,2}... | collective-permute-start | bytes 2752520 | tf_op jit(solution)/shard_map/ppermute | solution.py:32
  29.4 39.5 %collective-permute-start.2 = (bf16[3584,128]{1,0:T(8,128)(2,1)S(1)}, bf16[3584,128]{1,0:T(8,128)(2,1)}, u32[]{:S(2)}, u32[]{:S(2)}) collective-permute-start(bf16[3584,128]{1,0:T(8,128)(2,1)S(1)} %bitcast.43), channel_id=1, source_target_pairs={{48,0},{0,16},{16,32},{32,48},{49,1},{1,17},{17,33},{33,49},{50,2}... | collective-permute-start | bytes 2752520 | tf_op jit(solution)/shard_map/ppermute | solution.py:32
  46.9 39.3 %collective-permute-start.4 = (bf16[3584,128]{1,0:T(8,128)(2,1)}, bf16[3584,128]{1,0:T(8,128)(2,1)}, u32[]{:S(2)}, u32[]{:S(2)}) collective-permute-start(bf16[3584,128]{1,0:T(8,128)(2,1)} %collective-permute-done.3.before_g), channel_id=1, source_target_pairs={{48,0},{0,16},{16,32},{32,48},{49,1},{1,17},{17,33},{33,49},{50,2}... | collective-permute-start | bytes 2752520 | tf_op jit(solution)/shard_map/ppermute | solution.py:32
  48.8 38.9 %collective-permute-start.5 = (bf16[3584,128]{1,0:T(8,128)(2,1)}, bf16[3584,128]{1,0:T(8,128)(2,1)}, u32[]{:S(2)}, u32[]{:S(2)}) collective-permute-start(bf16[3584,128]{1,0:T(8,128)(2,1)} %collective-permute-done.1.after_u), channel_id=1, source_target_pairs={{16,0},{32,16},{48,32},{0,48},{17,1},{33,17},{49,33},{1,49},{18,2}... | collective-permute-start | bytes 2752520 | tf_op jit(solution)/shard_map/ppermute | solution.py:32
  67.9 0.9 copy-start.11
  68.9 46.8 %collective-permute-start.8 = (bf16[512,896]{1,0:T(8,128)(2,1)S(1)}, bf16[512,896]{1,0:T(8,128)(2,1)S(1)}, u32[]{:S(2)}, u32[]{:S(2)}) collective-permute-start(bf16[512,896]{1,0:T(8,128)(2,1)S(1)} %bitcast.18), channel_id=1, source_target_pairs={{48,0},{0,16},{16,32},{32,48},{49,1},{1,17},{17,33},{33,49},{50,2}... | collective-permute-start | bytes 2752520 | tf_op jit(solution)/shard_map/ppermute | solution.py:32
  70.8 44.9 %collective-permute-start.6 = (bf16[512,896]{1,0:T(8,128)(2,1)S(1)}, bf16[512,896]{1,0:T(8,128)(2,1)S(1)}, u32[]{:S(2)}, u32[]{:S(2)}) collective-permute-start(bf16[512,896]{1,0:T(8,128)(2,1)S(1)} %bitcast.19), channel_id=1, source_target_pairs={{16,0},{32,16},{48,32},{0,48},{17,1},{33,17},{49,33},{1,49},{18,2}... | collective-permute-start | bytes 2752520 | tf_op jit(solution)/shard_map/ppermute | solution.py:32
  87.7 34.4 %collective-permute-start.7 = (bf16[512,896]{1,0:T(8,128)(2,1)S(1)}, bf16[512,896]{1,0:T(8,128)(2,1)}, u32[]{:S(2)}, u32[]{:S(2)}) collective-permute-start(bf16[512,896]{1,0:T(8,128)(2,1)S(1)} %bitcast.20), channel_id=1, source_target_pairs={{32,0},{48,16},{0,32},{16,48},{33,1},{49,17},{1,33},{17,49},{34,2}... | collective-permute-start | bytes 2752520 | tf_op jit(solution)/shard_map/ppermute | solution.py:32
  122.1 0.7 copy-start.5
  122.8 0.7 copy-start.6
  123.5 52.9 %copy-start = (bf16[1,24,3584]{2,1,0:T(8,128)(2,1)S(1)}, bf16[1,24,3584]{2,1,0:T(8,128)(2,1)}, u32[]{:S(2)}) copy-start(bf16[1,24,3584]{2,1,0:T(8,128)(2,1)} %param.8) | copy-start | bytes 516100
  123.5 56.2 %copy-start.1 = (bf16[24,3584]{1,0:T(8,128)(2,1)S(1)}, bf16[24,3584]{1,0:T(8,128)(2,1)}, u32[]{:S(2)}) copy-start(bf16[24,3584]{1,0:T(8,128)(2,1)} %fed_ref.1) | copy-start | bytes 516100
  123.5 56.2 %copy-start.2 = (f32[1,3584]{1,0:T(1,128)S(1)}, f32[1,3584]{1,0:T(1,128)}, u32[]{:S(2)}) copy-start(f32[1,3584]{1,0:T(1,128)} %gain_ref.3) | copy-start | bytes 43012
  123.5 56.2 %copy-start.7 = (s32[2,1,24,2]{2,3,1,0:T(2,128)S(1)}, s32[2,1,24,2]{2,3,1,0:T(2,128)}, u32[]{:S(2)}) copy-start(s32[2,1,24,2]{2,3,1,0:T(2,128)} %param.10) | copy-start | bytes 1156
  123.5 56.2 %copy-start.8 = (f32[2,1,24,2]{2,3,1,0:T(2,128)S(1)}, f32[2,1,24,2]{2,3,1,0:T(2,128)}, u32[]{:S(2)}) copy-start(f32[2,1,24,2]{2,3,1,0:T(2,128)} %param.11) | copy-start | bytes 1156
  177.1 2.5 collective-permute-start.9
  275.5 0.7 copy-start.3
  276.3 0.7 copy-start.4
Sparse Core Ops, SparseCore 0:
  10.1 83.7 all-gather.4
  180.7 73.7 all-gather.6
